TPU v7x, 256 devices: a whole 4x4x8 slice. The times are simulated.
256 devices in a mesh: island: 16 (over y_hi, x, core), fsdp: 16 (over y_lo, z).
Axes of the slice: x: 4, y: 4 (y_hi: 2, y_lo: 2; y = y_hi * 2 + y_lo), z: 8, core: 2. Of those that a mesh axis runs over, the one named last changes fastest.
Arguments:
- inputs: bfloat16 [16, 4096, 8192], P('island', 'fsdp'), may hold values from -6 to 6
- cotangent: bfloat16 [16, 4096, 512], P('island', 'fsdp'), may hold values from -6 to 6
- key_weight: bfloat16 [16, 8192, 512], P('island', 'fsdp'), may hold values from -0.0625 to 0.0625
- pseudo_grads: bfloat16 [16, 8192, 512], P('island', 'fsdp'), may hold values from -3 to 3
- outer_params: float32 [8192, 512], P('fsdp'), may hold values from -6 to 6
- outer_momentum: float32 [8192, 512], P('fsdp'), may hold values from -3 to 3
Outputs:
- input_grads: bfloat16 [16, 4096, 8192], P('island', 'fsdp')
- weight_grads: float32 [16, 8192, 512], P('island', 'fsdp')
- new_params: float32 [8192, 512], P('fsdp')
- new_momentum: float32 [8192, 512], P('fsdp')
All inputs are finite; a program needn't handle non-finite values.
Results may differ from a plain program's by a relative error of at most 0.0055.
Values may be sent and summed in bfloat16 or wider, within the bound.
A program may use at most 128 MiB of HBM per device.

v0:
```python
import jax
import jax.numpy as jnp
from jax import lax
from jax.sharding import PartitionSpec as P

outer_rate = 0.7
outer_beta = 0.9


def body(inputs, cotangent, key_weight, pseudo_grads, outer_params, outer_momentum):
    island_terms = pseudo_grads[0].astype(jnp.float32)
    island_count = lax.axis_size("island")
    average = (
        lax.psum(island_terms.astype(jnp.bfloat16), "island").astype(jnp.float32) / island_count
    )
    new_momentum = outer_beta * outer_momentum + average
    new_params = outer_params - outer_rate * (average + outer_beta * new_momentum)
    features = inputs[0]
    cot_rows = cotangent[0]
    weight_rows = key_weight[0]
    token_total = features.shape[0] * lax.axis_size("fsdp")
    input_grad = lax.dot_general(
        cot_rows,
        lax.all_gather(weight_rows, "fsdp", axis=0, tiled=True),
        (((1,), (1,)), ((), ())),
        preferred_element_type=jnp.float32,
    ).astype(jnp.bfloat16)
    weight_grad = (
        lax.psum_scatter(
            lax.dot_general(
                features, cot_rows, (((0,), (0,)), ((), ())), preferred_element_type=jnp.float32
            ),
            "fsdp",
            scatter_dimension=0,
            tiled=True,
        )
        / token_total
    )
    return (input_grad[None], weight_grad[None], new_params, new_momentum)


def solution(mesh):
    return jax.shard_map(
        body,
        mesh=mesh,
        in_specs=(
            P("island", "fsdp", None),
            P("island", "fsdp", None),
            P("island", "fsdp", None),
            P("island", "fsdp", None),
            P("fsdp", None),
            P("fsdp", None),
        ),
        out_specs=(
            P("island", "fsdp", None),
            P("island", "fsdp", None),
            P("fsdp", None),
            P("fsdp", None),
        ),
        check_vma=False,
    )
```

profile of v0, /device:TPU:1, one launch (start us, length us, event | category | flops | bytes accessed | tf_op | source)
XLA Modules:
  0.0 313.5 jit_solution(12654219030113801698)
XLA Ops:
  8.0 0.0 copy-start
  8.0 0.0 all-reduce.2.cloned.1.call-start
  8.1 0.7 all-reduce.2.cloned.1.call-update
  8.7 0.0 all-gather.3.cloned.1.call-start
  8.8 0.5 all-gather.3.cloned.1.call-update
  9.3 0.0 reduce-scatter.2.cloned.1.call-start
  9.4 0.0 copy-done
  9.4 10.3 %fusion.2 = f32[8192,512]{1,0:T(8,128)} fusion(bf16[1,256,8192]{2,1,0:T(8,128)(2,1)} %param.6, bf16[1,256,512]{2,1,0:T(8,128)(2,1)S(1)} %copy-done), kind=kOutput, calls=%fused_computation.3 | convolution fusion | flops 2147483648 | bytes 21233664 | tf_op jit(solution)/shard_map/dot_general | solution.py:30
  19.7 0.0 copy-start.1
  19.7 0.0 copy-start.2
  19.7 0.0 reduce-scatter.2.cloned.1.call-update
  19.7 141.3 %all-reduce.2.cloned.1.call-done = bf16[512,512]{1,0:T(8,128)(2,1)} async-done(((bf16[512,512]{1,0:T(8,128)(2,1)}), bf16[512,512]{1,0:T(8,128)(2,1)}) %all-reduce.2.cloned.1.call-update) | async-done | bytes 524304 | tf_op jit(solution)/shard_map/psum | solution.py:14
  161.0 0.0 copy-done.1
  161.0 0.0 copy-done.2
  161.0 2.7 multiply_subtract_fusion
  163.7 0.0 all-gather.3.cloned.1.call-done
  163.7 7.9 %fusion = bf16[1,256,8192]{2,1,0:T(8,128)(2,1)} fusion(bf16[1,8192,512]{2,1,0:T(8,128)(2,1)} %all-gather.3.cloned.1.call-done, bf16[1,256,512]{2,1,0:T(8,128)(2,1)S(1)} %copy-done), kind=kOutput, calls=%fused_computation.1 | convolution fusion | flops 2149580800 | bytes 12845056 | tf_op jit(solution)/shard_map/dot_general | solution.py:22
  171.6 132.2 %reduce-scatter.2.cloned.1.call-done = f32[512,512]{1,0:T(8,128)} async-done(((f32[8192,512]{1,0:T(8,128)}), f32[512,512]{1,0:T(8,128)}) %reduce-scatter.2.cloned.1.call-update) | async-done | bytes 1048592 | tf_op jit(solution)/shard_map/reduce_scatter | solution.py:29
  303.8 2.3 multiply_bitcast_fusion
Async XLA Ops:
  8.0 1.4 copy-start
  8.0 153.0 %all-reduce.2.cloned.1.call-start = ((), (), s32[]{:S(2)}) async-start(), calls=%async_computation.2 | async-start | bytes 1048576 | tf_op jit(solution)/shard_map/psum | solution.py:14
  8.7 155.0 %all-gather.3.cloned.1.call-start = ((), (), s32[]{:S(2)}) async-start(), calls=%async_computation.3 | async-start | bytes 8912896 | tf_op jit(solution)/shard_map/all_gather | solution.py:24
  9.3 294.5 %reduce-scatter.2.cloned.1.call-start = ((), (), s32[]{:S(2)}) async-start(), calls=%async_computation.1 | async-start | bytes 17825792 | tf_op jit(solution)/shard_map/reduce_scatter | solution.py:29
  19.7 141.3 %copy-start.1 = (f32[512,512]{1,0:T(8,128)S(1)}, f32[512,512]{1,0:T(8,128)}, u32[]{:S(2)}) copy-start(f32[512,512]{1,0:T(8,128)} %param.10) | copy-start | bytes 3145732
  19.7 141.3 %copy-start.2 = (f32[512,512]{1,0:T(8,128)S(1)}, f32[512,512]{1,0:T(8,128)}, u32[]{:S(2)}) copy-start(f32[512,512]{1,0:T(8,128)} %param.11) | copy-start | bytes 3145732
Sparse Core Ops, SparseCore 0:
  11.5 149.4 all-reduce.1
Sparse Core Ops, SparseCore 1:
  11.0 107.7 all-gather.2
  121.1 182.6 reduce-scatter.1
where the time goes:
time: 314 us
  waiting for transfers between devices  275 us (88%)
  matrix products  18.2 us (6%)
  between operations  15.5 us (5%)
  other arithmetic  5 us (2%)
    psum x1, waiting for transfers between devices, body(): lax.psum(island_terms.astype(jnp.bfloat16), 'island').astype(jnp.float32)  141 us
    reduce_scatter x1, waiting for transfers between devices, body(): lax.psum_scatter(lax.dot_general(features, cot_rows, (((0,), (0,)), ((),...  132 us
    dot_general x1, matrix products, body(): lax.dot_general(features, cot_rows, (((0,), (0,)), ((), ())), preferred_e...  10.3 us
    dot_general x1, matrix products, body(): lax.dot_general(cot_rows, lax.all_gather(weight_rows, 'fsdp', axis=0, til...  7.87 us
  transfers between devices with their start and end apart: 3, of which 2 were waited for; matrix products, arithmetic and copies ran while one was open for 7% of the time, Pallas kernels for 0%

commit v1 on v0

v1 whole, which is shorter than its diff:
```python
import functools

import jax
import jax.numpy as jnp
from jax import lax
from jax.experimental import pallas as pl
from jax.experimental.pallas import tpu as pltpu
from jax.sharding import PartitionSpec as P

outer_rate = 0.7
outer_beta = 0.9

MESH = pl.DeviceIdType.MESH
F32 = jnp.float32
BF16 = jnp.bfloat16

Z = 8
PLANE = 8
ROWS = 512
HALF = ROWS // 2
TOK = 256
PURE = 128
HYB = ROWS - PURE
KW = 512
PIECE = ROWS // PLANE

UP, DOWN = 0, 1


def rows(start, size):
    return pl.ds(start, size)


def kernel(
    x_ref, c_ref, w_ref, pg_ref, op_ref, om_ref,
    ig_ref, wg_ref, np_ref, nm_ref,
    cot, xin, wb, term, rs_in, rs_out, ig_far, ig_own, ig_pure,
    pg_own, c_in, c_out, c_far, avg, opb, omb, npb, nmb, wgb,
    ag_s, ag_r, rs_s, rs_r, yx_s, yx_r, yc_s, yc_r, yw_s, yw_r, yi_s, yi_r,
    c1_s, c1_r, c2_s, c2_r, c3_s, c3_r, lx, lm, lo, lw,
):
    isl = lax.axis_index("island")
    fs = lax.axis_index("fsdp")
    z, yl = lax.rem(fs, Z), fs // Z
    q, yh = lax.rem(isl, PLANE), isl // PLANE
    up = (isl, yl * Z + lax.rem(z + 1, Z))
    down = (isl, yl * Z + lax.rem(z + Z - 1, Z))
    pair = (isl, (1 - yl) * Z + z)
    far = ((1 - yh) * PLANE + q, fs)
    plane = [(yh * PLANE + lax.rem(q + j, PLANE), fs) for j in range(1, PLANE)]
    ring = (up, down)

    barrier = pltpu.get_barrier_semaphore()
    for peer in [up, down, pair, far] + plane:
        pl.semaphore_signal(barrier, inc=1, device_id=peer, device_id_type=MESH)

    def remote(src, dst, ss, rs, peer):
        return pltpu.make_async_remote_copy(
            src_ref=src, dst_ref=dst, send_sem=ss, recv_sem=rs, device_id=peer, device_id_type=MESH
        )

    def columns(owner_yl, s):
        return pl.ds(pl.multiple_of((owner_yl * Z + lax.rem(z + s, Z)) * ROWS, ROWS), ROWS)

    local = [
        pltpu.make_async_copy(c_ref.at[0], cot.at[rows(0, TOK)], lm.at[0]),
        pltpu.make_async_copy(w_ref.at[0], wb.at[0, rows(0, ROWS)], lm.at[1]),
        pltpu.make_async_copy(
            pg_ref.at[0, pl.ds(pl.multiple_of(q * PIECE, PIECE), PIECE)], pg_own, lm.at[2]
        ),
        pltpu.make_async_copy(op_ref, opb, lm.at[3]),
        pltpu.make_async_copy(om_ref, omb, lm.at[4]),
    ]
    own_x = [
        pltpu.make_async_copy(x_ref.at[0, :, columns(yl, s)], xin.at[s, rows(0, TOK)], lx.at[s])
        for s in range(Z)
    ]
    for copy in local:
        copy.start()
    for s in (4, 3, 5, 2, 6, 1, 7, 0):
        own_x[s].start()

    y_w = remote(w_ref.at[0, rows(0, PURE)], wb.at[0, rows(ROWS, PURE)], yw_s, yw_r, pair)
    y_c = remote(c_ref.at[0], cot.at[rows(TOK, TOK)], yc_s, yc_r, pair)
    y_x = [
        remote(x_ref.at[0, :, columns(1 - yl, s)], xin.at[s, rows(TOK, TOK)], yx_s.at[s], yx_r.at[s], pair)
        for s in range(Z)
    ]

    cuts = {
        0: (0, HALF),
        1: (HALF, HALF),
        2: (ROWS, PURE),
        3: (ROWS, PURE // 2),
        4: (ROWS + PURE // 2, PURE // 2),
    }

    def slot(d, r):
        return r if d == UP else (Z - r) % Z

    def gather(d, r, c):
        start, size = cuts[c]
        src = w_ref.at[0, rows(start, size)] if r == 0 and c < 2 else wb.at[slot(d, r), rows(start, size)]
        dst = wb.at[slot(d, r + 1), rows(start, size)]
        n = min(c, 2)
        return remote(src, dst, ag_s.at[d, r, n], ag_r.at[d, r, n], ring[d])

    first = {UP: 0, DOWN: 1}
    last_pure = {UP: 3, DOWN: 4}

    c_1 = [
        remote(
            pg_ref.at[0, pl.ds(pl.multiple_of(lax.rem(q + j, PLANE) * PIECE, PIECE), PIECE)],
            c_in.at[j - 1], c1_s.at[j - 1], c1_r.at[j - 1], plane[j - 1],
        )
        for j in range(1, PLANE)
    ]
    c_2 = remote(c_out, c_far, c2_s, c2_r, far)
    own_piece = pl.ds(pl.multiple_of(q * PIECE, PIECE), PIECE)
    c_3 = [
        remote(avg.at[own_piece], avg.at[own_piece], c3_s.at[j - 1], c3_r.at[j - 1], plane[j - 1])
        for j in range(1, PLANE)
    ]

    def c_3_arrival(j):
        piece = pl.ds(pl.multiple_of(lax.rem(q + PLANE - j, PLANE) * PIECE, PIECE), PIECE)
        return remote(avg.at[piece], avg.at[piece], c3_s.at[j - 1], c3_r.at[j - 1], plane[j - 1])

    half_of = {UP: (0, 1), DOWN: (1, 0)}

    def reduce_copy(d, k, h):
        part = rows(h * HALF, HALF)
        return remote(
            rs_out.at[d, k - 1, part], rs_in.at[d, k - 1, part],
            rs_s.at[d, k - 1, h], rs_r.at[d, k - 1, h], ring[d],
        )

    def target(d, k):
        return k if d == UP else Z - k

    def send_sum(d, k, h, chained):
        part = rows(h * HALF, HALF)
        total = term[target(d, k), part, :]
        if chained:
            reduce_copy(d, k + 1, h).wait_recv()
            total = total + rs_in[d, k, part, :].astype(F32)
        rs_out[d, k - 1, part, :] = total.astype(BF16)
        reduce_copy(d, k, h).start()

    def make_term(s):
        own_x[s].wait()
        y_x[s].wait_recv()

        @pl.loop(0, ROWS // 256)
        def _(i):
            part = pl.ds(pl.multiple_of(i * 256, 256), 256)
            term[s, part, :] = lax.dot_general(
                xin[s, :, part], cot[...], (((0,), (0,)), ((), ())), preferred_element_type=F32
            )

    out_copies = []

    def ig_copy(r):
        cols = columns(yl, Z - r)
        mine = pltpu.make_async_copy(ig_own.at[r], ig_ref.at[0, :, cols], lo.at[0, r])
        start = pl.multiple_of(((1 - yl) * Z + lax.rem(z + Z - r, Z)) * ROWS, ROWS)
        pure = pltpu.make_async_copy(ig_pure.at[r], ig_ref.at[0, :, pl.ds(start, PURE)], lo.at[1, r])
        start = pl.multiple_of((yl * Z + lax.rem(z + Z - r, Z)) * ROWS + PURE, 128)
        sent = remote(
            ig_far.at[r], ig_ref.at[0, :, pl.ds(start, HYB)], yi_s.at[r], yi_r.at[r], pair
        )
        return mine, pure, sent

    def make_ig(r):
        transposed = (((1,), (1,)), ((), ()))
        ig_far[r] = lax.dot_general(
            cot[TOK:, :], wb[r, PURE:ROWS, :], transposed, preferred_element_type=F32
        ).astype(BF16)
        mine, pure, sent = ig_copy(r)
        sent.start()
        ig_own[r] = lax.dot_general(
            cot[:TOK, :], wb[r, :ROWS, :], transposed, preferred_element_type=F32
        ).astype(BF16)
        mine.start()
        ig_pure[r] = lax.dot_general(
            cot[:TOK, :], wb[r, ROWS:, :], transposed, preferred_element_type=F32
        ).astype(BF16)
        pure.start()

    def pass_on(r, i):
        for d in (UP, DOWN):
            c = 2 if i == 2 else (first[d] if i == 0 else 1 - first[d])
            gather(d, r, c).wait_recv()
            if r + 1 < 3:
                gather(d, r + 1, c).start()
            elif r + 1 == 3 and i == 0:
                gather(d, 3, c).start()
            elif r + 1 == 3 and i == 2:
                gather(d, 3, last_pure[d]).start()

    pl.semaphore_wait(barrier, 4 + len(plane))

    y_w.start()
    for d in (UP, DOWN):
        gather(d, 0, first[d]).start()
        gather(d, 0, 1 - first[d]).start()
    y_c.start()
    for s in (4, 3, 5, 2):
        y_x[s].start()
    for copy in c_1:
        copy.start()

    y_w.wait_recv()
    for d in (UP, DOWN):
        gather(d, 0, 2).start()
    pass_on(0, 0)
    for copy in local[:3]:
        copy.wait()
    total = pg_own[...].astype(F32)
    for j in range(1, PLANE):
        c_1[j - 1].wait_recv()
        total = total + c_in[j - 1].astype(F32)
    c_out[...] = total.astype(BF16)
    c_2.start()
    for s in (6, 1, 7, 0):
        y_x[s].start()
    y_c.wait_recv()
    make_ig(0)
    pass_on(0, 1)
    pass_on(0, 2)
    make_term(4)
    make_ig(1)
    make_ig(7)
    pass_on(1, 0)
    make_term(3)
    pass_on(1, 1)
    make_term(5)
    pass_on(1, 2)
    make_ig(2)
    make_ig(6)
    make_term(2)
    pass_on(2, 0)
    c_2.wait_recv()
    avg[own_piece, :] = (c_out[...].astype(F32) + c_far[...].astype(F32)) * (1.0 / 16)
    for copy in c_3:
        copy.start()
    make_term(6)
    pass_on(2, 1)
    pass_on(2, 2)
    for d in (UP, DOWN):
        send_sum(d, 4, half_of[d][0], False)
    for d in (UP, DOWN):
        send_sum(d, 3, half_of[d][1], False)
    make_ig(3)
    make_ig(5)
    make_term(1)
    for d in (UP, DOWN):
        gather(d, 3, first[d]).wait_recv()
        gather(d, 3, last_pure[d]).wait_recv()
    make_ig(4)
    make_term(7)
    for d in (UP, DOWN):
        send_sum(d, 3, half_of[d][0], True)
    make_term(0)
    for h in (1, 0):
        for d in (UP, DOWN):
            send_sum(d, 2, half_of[d][h], True)

    for copy in local[3:]:
        copy.wait()
    for j in range(1, PLANE):
        c_3_arrival(j).wait_recv()

    @pl.loop(0, ROWS // 64)
    def _(i):
        part = pl.ds(pl.multiple_of(i * 64, 64), 64)
        average = avg[part, :]
        momentum = outer_beta * omb[part, :] + average
        nmb[part, :] = momentum
        npb[part, :] = opb[part, :] - outer_rate * (average + outer_beta * momentum)

    outer = [
        pltpu.make_async_copy(npb, np_ref, lm.at[5]),
        pltpu.make_async_copy(nmb, nm_ref, lm.at[6]),
    ]
    for copy in outer:
        copy.start()

    for h in (1, 0):
        for d in (UP, DOWN):
            send_sum(d, 1, half_of[d][h], True)
    for d in (UP, DOWN):
        for h in (1, 0):
            reduce_copy(d, 1, half_of[d][h]).wait_recv()
    wg_copies = []
    for h in (0, 1):
        part = rows(h * HALF, HALF)
        wgb[part, :] = (
            term[0, part, :] + rs_in[UP, 0, part, :].astype(F32) + rs_in[DOWN, 0, part, :].astype(F32)
        ) * (1.0 / 4096)
        copy = pltpu.make_async_copy(wgb.at[part], wg_ref.at[0, part], lw.at[h])
        copy.start()
        wg_copies.append(copy)

    for r in range(Z):
        mine, pure, sent = ig_copy(r)
        mine.wait()
        pure.wait()
        sent.wait_send()
    for copy in outer + wg_copies:
        copy.wait()
    y_w.wait_send()
    y_c.wait_send()
    c_2.wait_send()
    for s in range(Z):
        y_x[s].wait_send()
    for j in range(1, PLANE):
        c_1[j - 1].wait_send()
        c_3[j - 1].wait_send()
    for d in (UP, DOWN):
        for r in range(3):
            for c in range(3):
                gather(d, r, c).wait_send()
        gather(d, 3, first[d]).wait_send()
        gather(d, 3, last_pure[d]).wait_send()
        reduce_copy(d, 4, half_of[d][0]).wait_send()
        for k in (3, 2, 1):
            for h in (0, 1):
                reduce_copy(d, k, h).wait_send()
    for r in range(Z):
        start = pl.multiple_of(((1 - yl) * Z + lax.rem(z + Z - r, Z)) * ROWS + PURE, 128)
        remote(
            ig_far.at[r], ig_ref.at[0, :, pl.ds(start, HYB)], yi_s.at[r], yi_r.at[r], pair
        ).wait_recv()


def body(inputs, cotangent, key_weight, pseudo_grads, outer_params, outer_momentum):
    dma = pltpu.SemaphoreType.DMA
    vmem = pltpu.VMEM
    anywhere = pl.BlockSpec(memory_space=pl.ANY)
    return pl.pallas_call(
        kernel,
        name="key_backward",
        out_shape=(
            jax.ShapeDtypeStruct((1, TOK, 2 * Z * ROWS), BF16),
            jax.ShapeDtypeStruct((1, ROWS, KW), F32),
            jax.ShapeDtypeStruct((ROWS, KW), F32),
            jax.ShapeDtypeStruct((ROWS, KW), F32),
        ),
        in_specs=[anywhere] * 6,
        out_specs=(anywhere,) * 4,
        scratch_shapes=[
            vmem((2 * TOK, KW), BF16),
            vmem((Z, 2 * TOK, ROWS), BF16),
            vmem((Z, ROWS + PURE, KW), BF16),
            vmem((Z, ROWS, KW), F32),
            vmem((2, 4, ROWS, KW), BF16),
            vmem((2, 4, ROWS, KW), BF16),
            vmem((Z, TOK, HYB), BF16),
            vmem((Z, TOK, ROWS), BF16),
            vmem((Z, TOK, PURE), BF16),
            vmem((PIECE, KW), BF16),
            vmem((PLANE - 1, PIECE, KW), BF16),
            vmem((PIECE, KW), BF16),
            vmem((PIECE, KW), BF16),
            vmem((ROWS, KW), F32),
            vmem((ROWS, KW), F32),
            vmem((ROWS, KW), F32),
            vmem((ROWS, KW), F32),
            vmem((ROWS, KW), F32),
            vmem((ROWS, KW), F32),
            dma((2, 4, 3)), dma((2, 4, 3)),
            dma((2, 4, 2)), dma((2, 4, 2)),
            dma((Z,)), dma((Z,)),
            dma, dma, dma, dma,
            dma((Z,)), dma((Z,)),
            dma((PLANE - 1,)), dma((PLANE - 1,)),
            dma, dma,
            dma((PLANE - 1,)), dma((PLANE - 1,)),
            dma((Z,)), dma((7,)), dma((2, Z)), dma((2,)),
        ],
        compiler_params=pltpu.CompilerParams(
            collective_id=0, has_side_effects=True, vmem_limit_bytes=56 * 2**20
        ),
        cost_estimate=pl.CostEstimate(
            flops=4 * TOK * 2 * Z * ROWS * KW, bytes_accessed=24 * 2**20, transcendentals=0
        ),
    )(inputs, cotangent, key_weight, pseudo_grads, outer_params, outer_momentum)


def solution(mesh):
    return jax.shard_map(
        body,
        mesh=mesh,
        in_specs=(
            P("island", "fsdp", None),
            P("island", "fsdp", None),
            P("island", "fsdp", None),
            P("island", "fsdp", None),
            P("fsdp", None),
            P("fsdp", None),
        ),
        out_specs=(
            P("island", "fsdp", None),
            P("island", "fsdp", None),
            P("fsdp", None),
            P("fsdp", None),
        ),
        check_vma=False,
    )
```

time: 314 us -> 111 us (0.35)
  waiting for transfers between devices: 275 us -> 0 us
  Pallas kernels: 0 us -> 102 us
  matrix products: 18.2 us -> 0 us
  between operations: 15.5 us -> 0.66 us
  local copies, waits for them, and re-layouts: 0.02 us -> 7.71 us
  other arithmetic: 5 us -> 0 us
    psum x1 -> x0, waiting for transfers between devices: 141 us -> none  [body(): lax.psum(island_terms.astype(jnp.bfloat16), 'island').astype(jnp.float32)]
    reduce_scatter x1 -> x0, waiting for transfers between devices: 132 us -> none  [body(): lax.psum_scatter(lax.dot_general(features, cot_rows, (((0,), (0,)), ((),...]
    pallas_call x0 -> x1, Pallas kernels: none -> 102 us  [body(): pl.pallas_call(kernel, name='key_backward', out_shape=(jax.ShapeDtypeStru...]
    dot_general x2 -> x0, matrix products: 18.2 us -> none  [the longest x1 10.3 us: body(): lax.dot_general(features, cot_rows, (((0,), (0,)), ((), ())), preferred_e...]
    unnamed x6 -> x10, local copies, waits for them, and re-layouts: 0.02 us -> 7.71 us
  transfers between devices with their start and end apart: 3 -> 0, of which waited for: 2 -> 0; matrix products, arithmetic and copies ran while one was open for 7% -> 0% of each run, Pallas kernels for 0% -> 0%
where the time goes in v1:
time: 111 us; the launch traced here: 110 us
  Pallas kernels  102 us (92%)
  local copies, waits for them, and re-layouts  7.71 us (7%)
    pallas_call x1, Pallas kernels, body(): pl.pallas_call(kernel, name='key_backward', out_shape=(jax.ShapeDtypeStru...  102 us
    unnamed x10, local copies, waits for them, and re-layouts  7.71 us

profile of v1, /device:TPU:1, one launch (start us, length us, event | category | flops | bytes accessed | tf_op | source)
XLA Modules:
  0.0 110.5 jit_solution(552339418945354568)
XLA Ops:
  0.6 102.1 %key_backward.1 = (bf16[1,256,8192]{2,1,0:T(8,128)(2,1)}, f32[1,512,512]{2,1,0:T(8,128)}, f32[512,512]{1,0:T(8,128)}, f32[512,512]{1,0:T(8,128)}) custom-call(bf16[1,256,8192]{2,1,0:T(8,128)(2,1)} %x_ref.1, bf16[1,256,512]{2,1,0:T(8,128)(2,1)} %c_ref.1, bf16[1,512,512]{2,1,0:T(8,128)(2,1)} %w_ref.1, bf16[1,512,512]{2,1,0:T(8,128)(2,1)} %pg_ref.1, ...), custom_call_target="tpu_custom_call" | custom-call | flops 4294967296 | bytes 25165824 | tf_op jit(solution)/shard_map/key_backward/pallas_call | solution.py:341
  102.7 0.0 copy-start.2
  102.7 0.0 copy-start.1
  102.8 4.8 %copy.14 = bf16[1,256,8192]{2,1,0:T(8,128)(2,1)} copy(bf16[1,256,8192]{2,1,0:T(8,128)(2,1)} %get-tuple-element.8) | data formatting | bytes 8388608
  107.5 0.0 copy-done.2
  107.5 0.0 copy-start
  107.5 1.0 copy.15
  108.5 0.0 copy-done.1
  108.5 1.0 copy.16
  109.5 0.0 copy-done
  109.5 1.0 copy.17
Async XLA Ops:
  102.7 4.8 %copy-start.2 = (f32[1,512,512]{2,1,0:T(8,128)S(1)}, f32[1,512,512]{2,1,0:T(8,128)}, u32[]{:S(2)}) copy-start(f32[1,512,512]{2,1,0:T(8,128)} %get-tuple-element.9) | copy-start | bytes 3145732
  102.7 5.8 %copy-start.1 = (f32[512,512]{1,0:T(8,128)S(1)}, f32[512,512]{1,0:T(8,128)}, u32[]{:S(2)}) copy-start(f32[512,512]{1,0:T(8,128)} %get-tuple-element.10) | copy-start | bytes 3145732
  107.5 1.9 %copy-start = (f32[512,512]{1,0:T(8,128)S(1)}, f32[512,512]{1,0:T(8,128)}, u32[]{:S(2)}) copy-start(f32[512,512]{1,0:T(8,128)} %get-tuple-element.11) | copy-start | bytes 3145732

commit v2 on v1

--- a/solution.py
+++ b/solution.py
@@ -34,10 +34,10 @@
 def kernel(
     x_ref, c_ref, w_ref, pg_ref, op_ref, om_ref,
     ig_ref, wg_ref, np_ref, nm_ref,
-    cot, xin, wb, term, rs_in, rs_out, ig_far, ig_own, ig_pure,
-    pg_own, c_in, c_out, c_far, avg, opb, omb, npb, nmb, wgb,
+    cot, xin, wb, term, rs_in, rs_out, ig_far,
+    pg_own, c_in, c_out, c_far, avg, opb, omb,
     ag_s, ag_r, rs_s, rs_r, yx_s, yx_r, yc_s, yc_r, yw_s, yw_r, yi_s, yi_r,
-    c1_s, c1_r, c2_s, c2_r, c3_s, c3_r, lx, lm, lo, lw,
+    c1_s, c1_r, c2_s, c2_r, c3_s, c3_r, lx, lm,
 ):
     isl = lax.axis_index("island")
     fs = lax.axis_index("fsdp")
@@ -158,34 +158,33 @@
                 xin[s, :, part], cot[...], (((0,), (0,)), ((), ())), preferred_element_type=F32
             )
 
-    out_copies = []
-
-    def ig_copy(r):
-        cols = columns(yl, Z - r)
-        mine = pltpu.make_async_copy(ig_own.at[r], ig_ref.at[0, :, cols], lo.at[0, r])
-        start = pl.multiple_of(((1 - yl) * Z + lax.rem(z + Z - r, Z)) * ROWS, ROWS)
-        pure = pltpu.make_async_copy(ig_pure.at[r], ig_ref.at[0, :, pl.ds(start, PURE)], lo.at[1, r])
-        start = pl.multiple_of((yl * Z + lax.rem(z + Z - r, Z)) * ROWS + PURE, 128)
-        sent = remote(
-            ig_far.at[r], ig_ref.at[0, :, pl.ds(start, HYB)], yi_s.at[r], yi_r.at[r], pair
+    def own_columns(r, start, size):
+        return pl.ds(pl.multiple_of((yl * Z + lax.rem(z + Z - r, Z)) * ROWS + start, 128), size)
+
+    def pair_columns(r, start, size):
+        return pl.ds(pl.multiple_of(((1 - yl) * Z + lax.rem(z + Z - r, Z)) * ROWS + start, 128), size)
+
+    def ig_sent(r):
+        return remote(
+            ig_far.at[r], ig_ref.at[0, :, own_columns(r, PURE, HYB)], yi_s.at[r], yi_r.at[r], pair
         )
-        return mine, pure, sent
+
+    def ig_arrival(r):
+        part = ig_ref.at[0, :, pair_columns(r, PURE, HYB)]
+        return remote(part, part, yi_s.at[r], yi_r.at[r], pair)
 
     def make_ig(r):
         transposed = (((1,), (1,)), ((), ()))
         ig_far[r] = lax.dot_general(
             cot[TOK:, :], wb[r, PURE:ROWS, :], transposed, preferred_element_type=F32
         ).astype(BF16)
-        mine, pure, sent = ig_copy(r)
-        sent.start()
-        ig_own[r] = lax.dot_general(
+        ig_sent(r).start()
+        ig_ref[0, :, own_columns(r, 0, ROWS)] = lax.dot_general(
             cot[:TOK, :], wb[r, :ROWS, :], transposed, preferred_element_type=F32
         ).astype(BF16)
-        mine.start()
-        ig_pure[r] = lax.dot_general(
+        ig_ref[0, :, pair_columns(r, 0, PURE)] = lax.dot_general(
             cot[:TOK, :], wb[r, ROWS:, :], transposed, preferred_element_type=F32
         ).astype(BF16)
-        pure.start()
 
     def pass_on(r, i):
         for d in (UP, DOWN):
@@ -276,15 +275,8 @@
         part = pl.ds(pl.multiple_of(i * 64, 64), 64)
         average = avg[part, :]
         momentum = outer_beta * omb[part, :] + average
-        nmb[part, :] = momentum
-        npb[part, :] = opb[part, :] - outer_rate * (average + outer_beta * momentum)
-
-    outer = [
-        pltpu.make_async_copy(npb, np_ref, lm.at[5]),
-        pltpu.make_async_copy(nmb, nm_ref, lm.at[6]),
-    ]
-    for copy in outer:
-        copy.start()
+        nm_ref[part, :] = momentum
+        np_ref[part, :] = opb[part, :] - outer_rate * (average + outer_beta * momentum)
 
     for h in (1, 0):
         for d in (UP, DOWN):
@@ -292,23 +284,14 @@
     for d in (UP, DOWN):
         for h in (1, 0):
             reduce_copy(d, 1, half_of[d][h]).wait_recv()
-    wg_copies = []
     for h in (0, 1):
         part = rows(h * HALF, HALF)
-        wgb[part, :] = (
+        wg_ref[0, part, :] = (
             term[0, part, :] + rs_in[UP, 0, part, :].astype(F32) + rs_in[DOWN, 0, part, :].astype(F32)
         ) * (1.0 / 4096)
-        copy = pltpu.make_async_copy(wgb.at[part], wg_ref.at[0, part], lw.at[h])
-        copy.start()
-        wg_copies.append(copy)
 
     for r in range(Z):
-        mine, pure, sent = ig_copy(r)
-        mine.wait()
-        pure.wait()
-        sent.wait_send()
-    for copy in outer + wg_copies:
-        copy.wait()
+        ig_sent(r).wait_send()
     y_w.wait_send()
     y_c.wait_send()
     c_2.wait_send()
@@ -328,27 +311,45 @@
             for h in (0, 1):
                 reduce_copy(d, k, h).wait_send()
     for r in range(Z):
-        start = pl.multiple_of(((1 - yl) * Z + lax.rem(z + Z - r, Z)) * ROWS + PURE, 128)
-        remote(
-            ig_far.at[r], ig_ref.at[0, :, pl.ds(start, HYB)], yi_s.at[r], yi_r.at[r], pair
-        ).wait_recv()
+        ig_arrival(r).wait_recv()
+
+
+def finish_kernel(a, b, c, d, a_out, b_out, c_out, d_out, sems):
+    copies = [pltpu.make_async_copy(x, y, sems.at[n]) for n, (x, y) in enumerate(
+        [(a, a_out), (b, b_out), (c, c_out), (d, d_out)])]
+    for copy in copies:
+        copy.start()
+    for copy in copies:
+        copy.wait()
+
+
+def finish(*arrays):
+    return pl.pallas_call(
+        finish_kernel,
+        name="finish",
+        out_shape=tuple(jax.ShapeDtypeStruct(x.shape, x.dtype) for x in arrays),
+        in_specs=[pl.BlockSpec(memory_space=pltpu.VMEM)] * 4,
+        out_specs=(pl.BlockSpec(memory_space=pltpu.HBM),) * 4,
+        scratch_shapes=[pltpu.SemaphoreType.DMA((4,))],
+        compiler_params=pltpu.CompilerParams(vmem_limit_bytes=2**20),
+    )(*[pltpu.with_memory_space_constraint(x, pltpu.VMEM) for x in arrays])
 
 
 def body(inputs, cotangent, key_weight, pseudo_grads, outer_params, outer_momentum):
     dma = pltpu.SemaphoreType.DMA
     vmem = pltpu.VMEM
-    anywhere = pl.BlockSpec(memory_space=pl.ANY)
-    return pl.pallas_call(
+    anywhere = pl.BlockSpec(memory_space=pltpu.HBM)
+    return finish(*pl.pallas_call(
         kernel,
         name="key_backward",
         out_shape=(
-            jax.ShapeDtypeStruct((1, TOK, 2 * Z * ROWS), BF16),
-            jax.ShapeDtypeStruct((1, ROWS, KW), F32),
-            jax.ShapeDtypeStruct((ROWS, KW), F32),
-            jax.ShapeDtypeStruct((ROWS, KW), F32),
+            vmem((1, TOK, 2 * Z * ROWS), BF16),
+            vmem((1, ROWS, KW), F32),
+            vmem((ROWS, KW), F32),
+            vmem((ROWS, KW), F32),
         ),
         in_specs=[anywhere] * 6,
-        out_specs=(anywhere,) * 4,
+        out_specs=(pl.BlockSpec(memory_space=vmem),) * 4,
         scratch_shapes=[
             vmem((2 * TOK, KW), BF16),
             vmem((Z, 2 * TOK, ROWS), BF16),
@@ -357,15 +358,10 @@
             vmem((2, 4, ROWS, KW), BF16),
             vmem((2, 4, ROWS, KW), BF16),
             vmem((Z, TOK, HYB), BF16),
-            vmem((Z, TOK, ROWS), BF16),
-            vmem((Z, TOK, PURE), BF16),
             vmem((PIECE, KW), BF16),
             vmem((PLANE - 1, PIECE, KW), BF16),
             vmem((PIECE, KW), BF16),
             vmem((PIECE, KW), BF16),
-            vmem((ROWS, KW), F32),
-            vmem((ROWS, KW), F32),
-            vmem((ROWS, KW), F32),
             vmem((ROWS, KW), F32),
             vmem((ROWS, KW), F32),
             vmem((ROWS, KW), F32),
@@ -377,15 +373,15 @@
             dma((PLANE - 1,)), dma((PLANE - 1,)),
             dma, dma,
             dma((PLANE - 1,)), dma((PLANE - 1,)),
-            dma((Z,)), dma((7,)), dma((2, Z)), dma((2,)),
+            dma((Z,)), dma((5,)),
         ],
         compiler_params=pltpu.CompilerParams(
-            collective_id=0, has_side_effects=True, vmem_limit_bytes=56 * 2**20
+            collective_id=0, has_side_effects=True, vmem_limit_bytes=54 * 2**20
         ),
         cost_estimate=pl.CostEstimate(
             flops=4 * TOK * 2 * Z * ROWS * KW, bytes_accessed=24 * 2**20, transcendentals=0
         ),
-    )(inputs, cotangent, key_weight, pseudo_grads, outer_params, outer_momentum)
+    )(inputs, cotangent, key_weight, pseudo_grads, outer_params, outer_momentum))
 
 
 def solution(mesh):

time: 111 us -> 105 us (0.946)
  local copies, waits for them, and re-layouts: 7.71 us -> 0 us
  Pallas kernels: 102 us -> 104 us
    unnamed x10 -> x0, local copies, waits for them, and re-layouts: 7.71 us -> none
    pallas_call x1 -> x2, Pallas kernels: 102 us -> 104 us  [the longest x1 101 us: body(): pl.pallas_call(kernel, name='key_backward', out_shape=(vmem((1, TOK, 2 *...]
where the time goes in v2:
time: 105 us
  Pallas kernels  104 us (99%)
    pallas_call x1, Pallas kernels, body(): pl.pallas_call(kernel, name='key_backward', out_shape=(vmem((1, TOK, 2 *...  101 us
    pallas_call x1, Pallas kernels, finish(): pl.pallas_call(finish_kernel, name='finish', out_shape=tuple((jax.ShapeDt...  3.02 us

profile of v2, /device:TPU:1, one launch (start us, length us, event | category | flops | bytes accessed | tf_op | source)
XLA Modules:
  0.0 104.7 jit_solution(8395279429544605617)
XLA Ops:
  0.6 101.0 %key_backward.1 = (bf16[1,256,8192]{2,1,0:T(8,128)(2,1)S(1)}, f32[1,512,512]{2,1,0:T(8,128)S(1)}, f32[512,512]{1,0:T(8,128)S(1)}, f32[512,512]{1,0:T(8,128)S(1)}) custom-call(bf16[1,256,8192]{2,1,0:T(8,128)(2,1)} %x_ref.1, bf16[1,256,512]{2,1,0:T(8,128)(2,1)} %c_ref.1, bf16[1,512,512]{2,1,0:T(8,128)(2,1)} %w_ref.1, bf16[1,512,512]{2,1,0:T(8,128)(2,1)} %pg_ref.1, ...), custom_call_target="tpu_custom_call" | custom-call | flops 4294967296 | bytes 25165824 | tf_op jit(solution)/shard_map/key_backward/pallas_call | solution.py:342
  101.7 3.0 %finish.1 = (bf16[1,256,8192]{2,1,0:T(8,128)(2,1)}, f32[1,512,512]{2,1,0:T(8,128)}, f32[512,512]{1,0:T(8,128)}, f32[512,512]{1,0:T(8,128)}) custom-call(bf16[1,256,8192]{2,1,0:T(8,128)(2,1)S(1)} %get-tuple-element.8.a, f32[1,512,512]{2,1,0:T(8,128)S(1)} %get-tuple-element.9.b, f32[512,512]{1,0:T(8,128)S(1)} %get-tuple-element.10.c, ...), custom_call_target="tpu_custom_call" | custom-call | tf_op jit(solution)/shard_map/finish/pallas_call | solution.py:327

commit v3 on v2

--- a/solution.py
+++ b/solution.py
@@ -34,7 +34,7 @@
 def kernel(
     x_ref, c_ref, w_ref, pg_ref, op_ref, om_ref,
     ig_ref, wg_ref, np_ref, nm_ref,
-    cot, xin, wb, term, rs_in, rs_out, ig_far,
+    cot, xin, wb, term, rs_in, rs_out, ig_far, ig_last,
     pg_own, c_in, c_out, c_far, avg, opb, omb,
     ag_s, ag_r, rs_s, rs_r, yx_s, yx_r, yc_s, yc_r, yw_s, yw_r, yi_s, yi_r,
     c1_s, c1_r, c2_s, c2_r, c3_s, c3_r, lx, lm,
@@ -75,11 +75,6 @@
         pltpu.make_async_copy(x_ref.at[0, :, columns(yl, s)], xin.at[s, rows(0, TOK)], lx.at[s])
         for s in range(Z)
     ]
-    for copy in local:
-        copy.start()
-    for s in (4, 3, 5, 2, 6, 1, 7, 0):
-        own_x[s].start()
-
     y_w = remote(w_ref.at[0, rows(0, PURE)], wb.at[0, rows(ROWS, PURE)], yw_s, yw_r, pair)
     y_c = remote(c_ref.at[0], cot.at[rows(TOK, TOK)], yc_s, yc_r, pair)
     y_x = [
@@ -91,8 +86,6 @@
         0: (0, HALF),
         1: (HALF, HALF),
         2: (ROWS, PURE),
-        3: (ROWS, PURE // 2),
-        4: (ROWS + PURE // 2, PURE // 2),
     }
 
     def slot(d, r):
@@ -102,11 +95,9 @@
         start, size = cuts[c]
         src = w_ref.at[0, rows(start, size)] if r == 0 and c < 2 else wb.at[slot(d, r), rows(start, size)]
         dst = wb.at[slot(d, r + 1), rows(start, size)]
-        n = min(c, 2)
-        return remote(src, dst, ag_s.at[d, r, n], ag_r.at[d, r, n], ring[d])
+        return remote(src, dst, ag_s.at[d, r, c], ag_r.at[d, r, c], ring[d])
 
     first = {UP: 0, DOWN: 1}
-    last_pure = {UP: 3, DOWN: 4}
 
     c_1 = [
         remote(
@@ -164,27 +155,34 @@
     def pair_columns(r, start, size):
         return pl.ds(pl.multiple_of(((1 - yl) * Z + lax.rem(z + Z - r, Z)) * ROWS + start, 128), size)
 
+    def far_part(r):
+        return (0, ROWS, ig_last) if r == 4 else (PURE, HYB, ig_far.at[r])
+
     def ig_sent(r):
+        start, size, src = far_part(r)
         return remote(
-            ig_far.at[r], ig_ref.at[0, :, own_columns(r, PURE, HYB)], yi_s.at[r], yi_r.at[r], pair
+            src, ig_ref.at[0, :, own_columns(r, start, size)], yi_s.at[r], yi_r.at[r], pair
         )
 
     def ig_arrival(r):
-        part = ig_ref.at[0, :, pair_columns(r, PURE, HYB)]
+        start, size, _ = far_part(r)
+        part = ig_ref.at[0, :, pair_columns(r, start, size)]
         return remote(part, part, yi_s.at[r], yi_r.at[r], pair)
 
     def make_ig(r):
         transposed = (((1,), (1,)), ((), ()))
-        ig_far[r] = lax.dot_general(
-            cot[TOK:, :], wb[r, PURE:ROWS, :], transposed, preferred_element_type=F32
+        start, size, far_ref = far_part(r)
+        far_ref[...] = lax.dot_general(
+            cot[TOK:, :], wb[r, start:ROWS, :], transposed, preferred_element_type=F32
         ).astype(BF16)
         ig_sent(r).start()
         ig_ref[0, :, own_columns(r, 0, ROWS)] = lax.dot_general(
             cot[:TOK, :], wb[r, :ROWS, :], transposed, preferred_element_type=F32
         ).astype(BF16)
-        ig_ref[0, :, pair_columns(r, 0, PURE)] = lax.dot_general(
-            cot[:TOK, :], wb[r, ROWS:, :], transposed, preferred_element_type=F32
-        ).astype(BF16)
+        if r != 4:
+            ig_ref[0, :, pair_columns(r, 0, PURE)] = lax.dot_general(
+                cot[:TOK, :], wb[r, ROWS:, :], transposed, preferred_element_type=F32
+            ).astype(BF16)
 
     def pass_on(r, i):
         for d in (UP, DOWN):
@@ -194,8 +192,6 @@
                 gather(d, r + 1, c).start()
             elif r + 1 == 3 and i == 0:
                 gather(d, 3, c).start()
-            elif r + 1 == 3 and i == 2:
-                gather(d, 3, last_pure[d]).start()
 
     pl.semaphore_wait(barrier, 4 + len(plane))
 
@@ -208,6 +204,10 @@
         y_x[s].start()
     for copy in c_1:
         copy.start()
+    for copy in local:
+        copy.start()
+    for s in (4, 3, 5, 2, 6, 1, 7, 0):
+        own_x[s].start()
 
     y_w.wait_recv()
     for d in (UP, DOWN):
@@ -255,7 +255,6 @@
     make_term(1)
     for d in (UP, DOWN):
         gather(d, 3, first[d]).wait_recv()
-        gather(d, 3, last_pure[d]).wait_recv()
     make_ig(4)
     make_term(7)
     for d in (UP, DOWN):
@@ -281,17 +280,7 @@
     for h in (1, 0):
         for d in (UP, DOWN):
             send_sum(d, 1, half_of[d][h], True)
-    for d in (UP, DOWN):
-        for h in (1, 0):
-            reduce_copy(d, 1, half_of[d][h]).wait_recv()
-    for h in (0, 1):
-        part = rows(h * HALF, HALF)
-        wg_ref[0, part, :] = (
-            term[0, part, :] + rs_in[UP, 0, part, :].astype(F32) + rs_in[DOWN, 0, part, :].astype(F32)
-        ) * (1.0 / 4096)
-
-    for r in range(Z):
-        ig_sent(r).wait_send()
+
     y_w.wait_send()
     y_c.wait_send()
     c_2.wait_send()
@@ -305,12 +294,28 @@
             for c in range(3):
                 gather(d, r, c).wait_send()
         gather(d, 3, first[d]).wait_send()
-        gather(d, 3, last_pure[d]).wait_send()
         reduce_copy(d, 4, half_of[d][0]).wait_send()
-        for k in (3, 2, 1):
+        for k in (3, 2):
             for h in (0, 1):
                 reduce_copy(d, k, h).wait_send()
-    for r in range(Z):
+    for r in (0, 1, 7, 2, 6):
+        ig_sent(r).wait_send()
+        ig_arrival(r).wait_recv()
+
+    for d in (UP, DOWN):
+        for h in (1, 0):
+            reduce_copy(d, 1, half_of[d][h]).wait_recv()
+    for h in (0, 1):
+        part = rows(h * HALF, HALF)
+        wg_ref[0, part, :] = (
+            term[0, part, :] + rs_in[UP, 0, part, :].astype(F32) + rs_in[DOWN, 0, part, :].astype(F32)
+        ) * (1.0 / 4096)
+
+    for d in (UP, DOWN):
+        for h in (0, 1):
+            reduce_copy(d, 1, h).wait_send()
+    for r in (3, 5, 4):
+        ig_sent(r).wait_send()
         ig_arrival(r).wait_recv()
 
 
@@ -358,6 +363,7 @@
             vmem((2, 4, ROWS, KW), BF16),
             vmem((2, 4, ROWS, KW), BF16),
             vmem((Z, TOK, HYB), BF16),
+            vmem((TOK, ROWS), BF16),
             vmem((PIECE, KW), BF16),
             vmem((PLANE - 1, PIECE, KW), BF16),
             vmem((PIECE, KW), BF16),

time: 105 us -> 103 us (0.981)
    pallas_call x1, Pallas kernels: 101 us -> 99.5 us  [body(): pl.pallas_call(kernel, name='key_backward', out_shape=(vmem((1, TOK, 2 *...]
where the time goes in v3:
time: 103 us
  Pallas kernels  103 us (100%)
    pallas_call x1, Pallas kernels, body(): pl.pallas_call(kernel, name='key_backward', out_shape=(vmem((1, TOK, 2 *...  99.5 us
    pallas_call x1, Pallas kernels, finish(): pl.pallas_call(finish_kernel, name='finish', out_shape=tuple((jax.ShapeDt...  3.02 us

profile of v3, /device:TPU:1, one launch (start us, length us, event | category | flops | bytes accessed | tf_op | source)
XLA Modules:
  0.0 103.2 jit_solution(332146401052174125)
XLA Ops:
  0.6 99.5 %key_backward.1 = (bf16[1,256,8192]{2,1,0:T(8,128)(2,1)S(1)}, f32[1,512,512]{2,1,0:T(8,128)S(1)}, f32[512,512]{1,0:T(8,128)S(1)}, f32[512,512]{1,0:T(8,128)S(1)}) custom-call(bf16[1,256,8192]{2,1,0:T(8,128)(2,1)} %x_ref.1, bf16[1,256,512]{2,1,0:T(8,128)(2,1)} %c_ref.1, bf16[1,512,512]{2,1,0:T(8,128)(2,1)} %w_ref.1, bf16[1,512,512]{2,1,0:T(8,128)(2,1)} %pg_ref.1, ...), custom_call_target="tpu_custom_call" | custom-call | flops 4294967296 | bytes 25165824 | tf_op jit(solution)/shard_map/key_backward/pallas_call | solution.py:347
  100.2 3.0 %finish.1 = (bf16[1,256,8192]{2,1,0:T(8,128)(2,1)}, f32[1,512,512]{2,1,0:T(8,128)}, f32[512,512]{1,0:T(8,128)}, f32[512,512]{1,0:T(8,128)}) custom-call(bf16[1,256,8192]{2,1,0:T(8,128)(2,1)S(1)} %get-tuple-element.8.a, f32[1,512,512]{2,1,0:T(8,128)S(1)} %get-tuple-element.9.b, f32[512,512]{1,0:T(8,128)S(1)} %get-tuple-element.10.c, ...), custom_call_target="tpu_custom_call" | custom-call | tf_op jit(solution)/shard_map/finish/pallas_call | solution.py:332

commit v4 on v3

--- a/solution.py
+++ b/solution.py
@@ -25,6 +25,8 @@
 PIECE = ROWS // PLANE
 
 UP, DOWN = 0, 1
+ISLANDS = 2 * PLANE
+ROOT = 1
 
 
 def rows(start, size):
@@ -37,7 +39,7 @@
     cot, xin, wb, term, rs_in, rs_out, ig_far, ig_last,
     pg_own, c_in, c_out, c_far, avg, opb, omb,
     ag_s, ag_r, rs_s, rs_r, yx_s, yx_r, yc_s, yc_r, yw_s, yw_r, yi_s, yi_r,
-    c1_s, c1_r, c2_s, c2_r, c3_s, c3_r, lx, lm,
+    c1_s, c1_r, c2_s, c2_r, c3_s, c3_r, lx, lm, below, here, all_in,
 ):
     isl = lax.axis_index("island")
     fs = lax.axis_index("fsdp")
@@ -51,8 +53,15 @@
     ring = (up, down)
 
     barrier = pltpu.get_barrier_semaphore()
-    for peer in [up, down, pair, far] + plane:
+    for peer in (down, pair):
         pl.semaphore_signal(barrier, inc=1, device_id=peer, device_id_type=MESH)
+
+    @pl.when(isl == ROOT)
+    def _():
+        for j in range(1, ISLANDS):
+            pl.semaphore_signal(
+                barrier, inc=1, device_id=(lax.rem(isl + j, ISLANDS), fs), device_id_type=MESH
+            )
 
     def remote(src, dst, ss, rs, peer):
         return pltpu.make_async_remote_copy(
@@ -193,22 +202,41 @@
             elif r + 1 == 3 and i == 0:
                 gather(d, 3, c).start()
 
-    pl.semaphore_wait(barrier, 4 + len(plane))
-
+    pl.semaphore_wait(barrier, jnp.where(isl == ROOT, 2, 3))
+    pl.semaphore_signal(below, inc=1, device_id=up, device_id_type=MESH)
     y_w.start()
-    for d in (UP, DOWN):
-        gather(d, 0, first[d]).start()
-        gather(d, 0, 1 - first[d]).start()
+    gather(UP, 0, first[UP]).start()
+    gather(UP, 0, 1 - first[UP]).start()
     y_c.start()
     for s in (4, 3, 5, 2):
         y_x[s].start()
-    for copy in c_1:
-        copy.start()
+
+    @pl.when(isl != ROOT)
+    def _():
+        pl.semaphore_signal(here, inc=1, device_id=(ROOT, fs), device_id_type=MESH)
+
     for copy in local:
         copy.start()
     for s in (4, 3, 5, 2, 6, 1, 7, 0):
         own_x[s].start()
-
+    pl.semaphore_wait(below, 1)
+    gather(DOWN, 0, first[DOWN]).start()
+    gather(DOWN, 0, 1 - first[DOWN]).start()
+
+    @pl.when(isl == ROOT)
+    def _():
+        pl.semaphore_wait(here, ISLANDS - 1)
+        for j in range(1, ISLANDS):
+            pl.semaphore_signal(
+                all_in, inc=1, device_id=(lax.rem(isl + j, ISLANDS), fs), device_id_type=MESH
+            )
+
+    @pl.when(isl != ROOT)
+    def _():
+        pl.semaphore_wait(all_in, 1)
+
+    for copy in c_1:
+        copy.start()
     y_w.wait_recv()
     for d in (UP, DOWN):
         gather(d, 0, 2).start()
@@ -380,6 +408,9 @@
             dma, dma,
             dma((PLANE - 1,)), dma((PLANE - 1,)),
             dma((Z,)), dma((5,)),
+            pltpu.SemaphoreType.REGULAR,
+            pltpu.SemaphoreType.REGULAR,
+            pltpu.SemaphoreType.REGULAR,
         ],
         compiler_params=pltpu.CompilerParams(
             collective_id=0, has_side_effects=True, vmem_limit_bytes=54 * 2**20

time: 103 us -> 101 us (0.981)
  Pallas kernels: 103 us -> 100 us
    pallas_call x1, Pallas kernels: 99.5 us -> 96.9 us  [body(): pl.pallas_call(kernel, name='key_backward', out_shape=(vmem((1, TOK, 2 *...]
where the time goes in v4:
time: 101 us
  Pallas kernels  100 us (99%)
    pallas_call x1, Pallas kernels, body(): pl.pallas_call(kernel, name='key_backward', out_shape=(vmem((1, TOK, 2 *...  96.9 us
    pallas_call x1, Pallas kernels, finish(): pl.pallas_call(finish_kernel, name='finish', out_shape=tuple((jax.ShapeDt...  3.02 us

profile of v4, /device:TPU:1, one launch (start us, length us, event | category | flops | bytes accessed | tf_op | source)
XLA Modules:
  0.0 100.6 jit_solution(12130405151604862727)
XLA Ops:
  0.6 96.9 %key_backward.1 = (bf16[1,256,8192]{2,1,0:T(8,128)(2,1)S(1)}, f32[1,512,512]{2,1,0:T(8,128)S(1)}, f32[512,512]{1,0:T(8,128)S(1)}, f32[512,512]{1,0:T(8,128)S(1)}) custom-call(bf16[1,256,8192]{2,1,0:T(8,128)(2,1)} %x_ref.1, bf16[1,256,512]{2,1,0:T(8,128)(2,1)} %c_ref.1, bf16[1,512,512]{2,1,0:T(8,128)(2,1)} %w_ref.1, bf16[1,512,512]{2,1,0:T(8,128)(2,1)} %pg_ref.1, ...), custom_call_target="tpu_custom_call" | custom-call | flops 4294967296 | bytes 25165824 | tf_op jit(solution)/shard_map/key_backward/pallas_call | solution.py:375
  97.6 3.0 %finish.1 = (bf16[1,256,8192]{2,1,0:T(8,128)(2,1)}, f32[1,512,512]{2,1,0:T(8,128)}, f32[512,512]{1,0:T(8,128)}, f32[512,512]{1,0:T(8,128)}) custom-call(bf16[1,256,8192]{2,1,0:T(8,128)(2,1)S(1)} %get-tuple-element.8.a, f32[1,512,512]{2,1,0:T(8,128)S(1)} %get-tuple-element.9.b, f32[512,512]{1,0:T(8,128)S(1)} %get-tuple-element.10.c, ...), custom_call_target="tpu_custom_call" | custom-call | tf_op jit(solution)/shard_map/finish/pallas_call | solution.py:360

commit v5 on v3

--- a/solution.py
+++ b/solution.py
@@ -25,6 +25,9 @@
 PIECE = ROWS // PLANE
 
 UP, DOWN = 0, 1
+ISLANDS = 2 * PLANE
+SIDE = 96
+ROOT = 1
 
 
 def rows(start, size):
@@ -37,7 +40,7 @@
     cot, xin, wb, term, rs_in, rs_out, ig_far, ig_last,
     pg_own, c_in, c_out, c_far, avg, opb, omb,
     ag_s, ag_r, rs_s, rs_r, yx_s, yx_r, yc_s, yc_r, yw_s, yw_r, yi_s, yi_r,
-    c1_s, c1_r, c2_s, c2_r, c3_s, c3_r, lx, lm,
+    c1_s, c1_r, c2_s, c2_r, c3_s, c3_r, lx, lm, above, below, pair_in, here, all_in,
 ):
     isl = lax.axis_index("island")
     fs = lax.axis_index("fsdp")
@@ -51,8 +54,21 @@
     ring = (up, down)
 
     barrier = pltpu.get_barrier_semaphore()
-    for peer in [up, down, pair, far] + plane:
-        pl.semaphore_signal(barrier, inc=1, device_id=peer, device_id_type=MESH)
+    def greet(sem, peer):
+        pl.semaphore_signal(sem, inc=1, device_id=peer, device_id_type=MESH)
+
+    pl.when(yl == 0)(lambda: greet(barrier, pair))
+    greet(barrier, (isl, fs))
+    pl.when(z < Z - 1)(lambda: greet(barrier, up))
+    pl.when(z == 0)(lambda: greet(barrier, down))
+
+    @pl.when(isl == ROOT)
+    def _():
+        for j in range(1, ISLANDS):
+            greet(barrier, (lax.rem(isl + j, ISLANDS), fs))
+
+    def count(condition):
+        return jnp.where(condition, 1, 0)
 
     def remote(src, dst, ss, rs, peer):
         return pltpu.make_async_remote_copy(
@@ -98,6 +114,35 @@
         return remote(src, dst, ag_s.at[d, r, c], ag_r.at[d, r, c], ring[d])
 
     first = {UP: 0, DOWN: 1}
+
+    last_hop = {
+        UP: (
+            (0, HALF - SIDE, None, None),
+            (HALF - SIDE, SIDE, z < Z - 1, z > 0),
+            (HALF, SIDE, z == Z - 2, z == Z - 1),
+        ),
+        DOWN: (
+            (HALF + SIDE, HALF - SIDE, None, None),
+            (HALF, SIDE, z > 0, z < Z - 1),
+            (HALF - SIDE, SIDE, z == 1, z == 0),
+        ),
+    }
+
+    def fourth(d, c):
+        start, size = last_hop[d][c][:2]
+        return remote(
+            wb.at[slot(d, 3), rows(start, size)], wb.at[4, rows(start, size)],
+            ag_s.at[d, 3, c], ag_r.at[d, 3, c], ring[d],
+        )
+
+    def only(condition, action):
+        if condition is None:
+            action()
+        else:
+            pl.when(condition)(action)
+
+    def fourth_start(d, c):
+        only(last_hop[d][c][2], lambda: fourth(d, c).start())
 
     c_1 = [
         remote(
@@ -190,25 +235,54 @@
             gather(d, r, c).wait_recv()
             if r + 1 < 3:
                 gather(d, r + 1, c).start()
-            elif r + 1 == 3 and i == 0:
-                gather(d, 3, c).start()
-
-    pl.semaphore_wait(barrier, 4 + len(plane))
-
-    y_w.start()
-    for d in (UP, DOWN):
+            elif i == 0:
+                fourth_start(d, 0)
+                fourth_start(d, 1)
+            elif i == 1:
+                fourth_start(d, 2)
+
+    pl.semaphore_wait(
+        barrier, 1 + count(z > 0) + count(z == Z - 1) + count(yl == 1) + count(isl != ROOT)
+    )
+    pl.when(yl == 1)(lambda: greet(pair_in, pair))
+    pl.when(z > 0)(lambda: greet(above, down))
+    pl.when(z == Z - 1)(lambda: greet(below, up))
+
+    def start_gather(d):
         gather(d, 0, first[d]).start()
         gather(d, 0, 1 - first[d]).start()
+
+    pl.when(yl == 0)(lambda: pl.semaphore_wait(pair_in, 1))
+    y_w.start()
     y_c.start()
+    pl.when(z > 0)(lambda: start_gather(DOWN))
     for s in (4, 3, 5, 2):
         y_x[s].start()
-    for copy in c_1:
-        copy.start()
+    pl.when(z < Z - 1)(lambda: pl.semaphore_wait(above, 1))
+    start_gather(UP)
+    pl.when(isl != ROOT)(lambda: greet(here, (ROOT, fs)))
     for copy in local:
         copy.start()
     for s in (4, 3, 5, 2, 6, 1, 7, 0):
         own_x[s].start()
 
+    @pl.when(z == 0)
+    def _():
+        pl.semaphore_wait(below, 1)
+        start_gather(DOWN)
+
+    @pl.when(isl == ROOT)
+    def _():
+        pl.semaphore_wait(here, ISLANDS - 1)
+        for j in range(1, ISLANDS):
+            greet(all_in, (lax.rem(isl + j, ISLANDS), fs))
+
+    @pl.when(isl != ROOT)
+    def _():
+        pl.semaphore_wait(all_in, 1)
+
+    for copy in c_1:
+        copy.start()
     y_w.wait_recv()
     for d in (UP, DOWN):
         gather(d, 0, 2).start()
@@ -254,7 +328,8 @@
     make_ig(5)
     make_term(1)
     for d in (UP, DOWN):
-        gather(d, 3, first[d]).wait_recv()
+        for c in range(3):
+            only(last_hop[d][c][3], fourth(d, c).wait_recv)
     make_ig(4)
     make_term(7)
     for d in (UP, DOWN):
@@ -293,7 +368,8 @@
         for r in range(3):
             for c in range(3):
                 gather(d, r, c).wait_send()
-        gather(d, 3, first[d]).wait_send()
+        for c in range(3):
+            only(last_hop[d][c][2], fourth(d, c).wait_send)
         reduce_copy(d, 4, half_of[d][0]).wait_send()
         for k in (3, 2):
             for h in (0, 1):
@@ -302,14 +378,16 @@
         ig_sent(r).wait_send()
         ig_arrival(r).wait_recv()
 
-    for d in (UP, DOWN):
-        for h in (1, 0):
-            reduce_copy(d, 1, half_of[d][h]).wait_recv()
-    for h in (0, 1):
-        part = rows(h * HALF, HALF)
-        wg_ref[0, part, :] = (
-            term[0, part, :] + rs_in[UP, 0, part, :].astype(F32) + rs_in[DOWN, 0, part, :].astype(F32)
-        ) * (1.0 / 4096)
+    for last in (False, True):
+        for d in (UP, DOWN):
+            h = half_of[d][0 if last else 1]
+            reduce_copy(d, 1, h).wait_recv()
+            part = rows(h * HALF, HALF)
+            arrived = rs_in[d, 0, part, :].astype(F32)
+            if last:
+                wg_ref[0, part, :] = (wg_ref[0, part, :] + arrived) * (1.0 / 4096)
+            else:
+                wg_ref[0, part, :] = term[0, part, :] + arrived
 
     for d in (UP, DOWN):
         for h in (0, 1):
@@ -380,7 +458,8 @@
             dma, dma,
             dma((PLANE - 1,)), dma((PLANE - 1,)),
             dma((Z,)), dma((5,)),
-        ],
+        ]
+        + [pltpu.SemaphoreType.REGULAR] * 5,
         compiler_params=pltpu.CompilerParams(
             collective_id=0, has_side_effects=True, vmem_limit_bytes=54 * 2**20
         ),

time: 103 us -> 99.5 us (0.966); the launches traced: 103 us -> 98.6 us
  Pallas kernels: 103 us -> 97.9 us
    pallas_call x1, Pallas kernels: 99.5 us -> 94.9 us  [body(): pl.pallas_call(kernel, name='key_backward', out_shape=(vmem((1, TOK, 2 *...]
where the time goes in v5:
time: 99.5 us; the launch traced here: 98.6 us
  Pallas kernels  97.9 us (98%)
    pallas_call x1, Pallas kernels, body(): pl.pallas_call(kernel, name='key_backward', out_shape=(vmem((1, TOK, 2 *...  94.9 us
    pallas_call x1, Pallas kernels, finish(): pl.pallas_call(finish_kernel, name='finish', out_shape=tuple((jax.ShapeDt...  3.02 us

profile of v5, /device:TPU:1, one launch (start us, length us, event | category | flops | bytes accessed | tf_op | source)
XLA Modules:
  0.0 98.6 jit_solution(31671552369530534)
XLA Ops:
  0.6 94.9 %key_backward.1 = (bf16[1,256,8192]{2,1,0:T(8,128)(2,1)S(1)}, f32[1,512,512]{2,1,0:T(8,128)S(1)}, f32[512,512]{1,0:T(8,128)S(1)}, f32[512,512]{1,0:T(8,128)S(1)}) custom-call(bf16[1,256,8192]{2,1,0:T(8,128)(2,1)} %x_ref.1, bf16[1,256,512]{2,1,0:T(8,128)(2,1)} %c_ref.1, bf16[1,512,512]{2,1,0:T(8,128)(2,1)} %w_ref.1, bf16[1,512,512]{2,1,0:T(8,128)(2,1)} %pg_ref.1, ...), custom_call_target="tpu_custom_call" | custom-call | flops 4294967296 | bytes 25165824 | tf_op jit(solution)/shard_map/key_backward/pallas_call | solution.py:425
  95.6 3.0 %finish.1 = (bf16[1,256,8192]{2,1,0:T(8,128)(2,1)}, f32[1,512,512]{2,1,0:T(8,128)}, f32[512,512]{1,0:T(8,128)}, f32[512,512]{1,0:T(8,128)}) custom-call(bf16[1,256,8192]{2,1,0:T(8,128)(2,1)S(1)} %get-tuple-element.8.a, f32[1,512,512]{2,1,0:T(8,128)S(1)} %get-tuple-element.9.b, f32[512,512]{1,0:T(8,128)S(1)} %get-tuple-element.10.c, ...), custom_call_target="tpu_custom_call" | custom-call | tf_op jit(solution)/shard_map/finish/pallas_call | solution.py:410

commit v6 on v5

--- a/solution.py
+++ b/solution.py
@@ -20,7 +20,6 @@
 HALF = ROWS // 2
 TOK = 256
 PURE = 128
-HYB = ROWS - PURE
 KW = 512
 PIECE = ROWS // PLANE
 
@@ -37,10 +36,11 @@
 def kernel(
     x_ref, c_ref, w_ref, pg_ref, op_ref, om_ref,
     ig_ref, wg_ref, np_ref, nm_ref,
-    cot, xin, wb, term, rs_in, rs_out, ig_far, ig_last,
+    cot, xin, wb, term, rs_in, rs_out, ig_far,
     pg_own, c_in, c_out, c_far, avg, opb, omb,
-    ag_s, ag_r, rs_s, rs_r, yx_s, yx_r, yc_s, yc_r, yw_s, yw_r, yi_s, yi_r,
-    c1_s, c1_r, c2_s, c2_r, c3_s, c3_r, lx, lm, above, below, pair_in, here, all_in,
+    y_s, ag_s, ag4_s, rs_s, c1_s, c3_s,
+    ag_r, rs_r, yx_r, yc_r, yw_r, yi_r, c1_r, c2_r, c3_r,
+    lx, lm, above, below, pair_in, here, all_in,
 ):
     isl = lax.axis_index("island")
     fs = lax.axis_index("fsdp")
@@ -62,10 +62,15 @@
     pl.when(z < Z - 1)(lambda: greet(barrier, up))
     pl.when(z == 0)(lambda: greet(barrier, down))
 
-    @pl.when(isl == ROOT)
+    root = (yh * PLANE + ROOT, fs)
+    low_root = isl == ROOT
+    high_root = isl == PLANE + ROOT
+
+    @pl.when(q == ROOT)
     def _():
-        for j in range(1, ISLANDS):
-            greet(barrier, (lax.rem(isl + j, ISLANDS), fs))
+        for peer in plane:
+            greet(barrier, peer)
+        pl.when(yh == 0)(lambda: greet(barrier, far))
 
     def count(condition):
         return jnp.where(condition, 1, 0)
@@ -79,22 +84,22 @@
         return pl.ds(pl.multiple_of((owner_yl * Z + lax.rem(z + s, Z)) * ROWS, ROWS), ROWS)
 
     local = [
-        pltpu.make_async_copy(c_ref.at[0], cot.at[rows(0, TOK)], lm.at[0]),
-        pltpu.make_async_copy(w_ref.at[0], wb.at[0, rows(0, ROWS)], lm.at[1]),
+        pltpu.make_async_copy(c_ref.at[0], cot.at[rows(0, TOK)], lm),
+        pltpu.make_async_copy(w_ref.at[0], wb.at[0, rows(0, ROWS)], lm),
         pltpu.make_async_copy(
-            pg_ref.at[0, pl.ds(pl.multiple_of(q * PIECE, PIECE), PIECE)], pg_own, lm.at[2]
-        ),
-        pltpu.make_async_copy(op_ref, opb, lm.at[3]),
-        pltpu.make_async_copy(om_ref, omb, lm.at[4]),
+            pg_ref.at[0, pl.ds(pl.multiple_of(q * PIECE, PIECE), PIECE)], pg_own, lm
+        ),
+        pltpu.make_async_copy(op_ref, opb, lm),
+        pltpu.make_async_copy(om_ref, omb, lm),
     ]
     own_x = [
-        pltpu.make_async_copy(x_ref.at[0, :, columns(yl, s)], xin.at[s, rows(0, TOK)], lx.at[s])
+        pltpu.make_async_copy(x_ref.at[0, :, columns(yl, s)], xin.at[s, rows(0, TOK)], lx)
         for s in range(Z)
     ]
-    y_w = remote(w_ref.at[0, rows(0, PURE)], wb.at[0, rows(ROWS, PURE)], yw_s, yw_r, pair)
-    y_c = remote(c_ref.at[0], cot.at[rows(TOK, TOK)], yc_s, yc_r, pair)
+    y_w = remote(w_ref.at[0, rows(0, PURE)], wb.at[0, rows(ROWS, PURE)], y_s, yw_r, pair)
+    y_c = remote(c_ref.at[0], cot.at[rows(TOK, TOK)], y_s, yc_r, pair)
     y_x = [
-        remote(x_ref.at[0, :, columns(1 - yl, s)], xin.at[s, rows(TOK, TOK)], yx_s.at[s], yx_r.at[s], pair)
+        remote(x_ref.at[0, :, columns(1 - yl, s)], xin.at[s, rows(TOK, TOK)], y_s, yx_r.at[s], pair)
         for s in range(Z)
     ]
 
@@ -111,7 +116,7 @@
         start, size = cuts[c]
         src = w_ref.at[0, rows(start, size)] if r == 0 and c < 2 else wb.at[slot(d, r), rows(start, size)]
         dst = wb.at[slot(d, r + 1), rows(start, size)]
-        return remote(src, dst, ag_s.at[d, r, c], ag_r.at[d, r, c], ring[d])
+        return remote(src, dst, ag_s, ag_r.at[d, r, c], ring[d])
 
     first = {UP: 0, DOWN: 1}
 
@@ -132,7 +137,7 @@
         start, size = last_hop[d][c][:2]
         return remote(
             wb.at[slot(d, 3), rows(start, size)], wb.at[4, rows(start, size)],
-            ag_s.at[d, 3, c], ag_r.at[d, 3, c], ring[d],
+            ag4_s.at[d, c], ag_r.at[d, 3, c], ring[d],
         )
 
     def only(condition, action):
@@ -147,20 +152,28 @@
     c_1 = [
         remote(
             pg_ref.at[0, pl.ds(pl.multiple_of(lax.rem(q + j, PLANE) * PIECE, PIECE), PIECE)],
-            c_in.at[j - 1], c1_s.at[j - 1], c1_r.at[j - 1], plane[j - 1],
+            c_in.at[j - 1], c1_s, c1_r, plane[j - 1],
         )
         for j in range(1, PLANE)
     ]
-    c_2 = remote(c_out, c_far, c2_s, c2_r, far)
+    c_2 = remote(c_out, c_far, y_s, c2_r, far)
     own_piece = pl.ds(pl.multiple_of(q * PIECE, PIECE), PIECE)
     c_3 = [
-        remote(avg.at[own_piece], avg.at[own_piece], c3_s.at[j - 1], c3_r.at[j - 1], plane[j - 1])
+        remote(avg.at[own_piece], avg.at[own_piece], c3_s, c3_r, plane[j - 1])
         for j in range(1, PLANE)
     ]
 
-    def c_3_arrival(j):
-        piece = pl.ds(pl.multiple_of(lax.rem(q + PLANE - j, PLANE) * PIECE, PIECE), PIECE)
-        return remote(avg.at[piece], avg.at[piece], c3_s.at[j - 1], c3_r.at[j - 1], plane[j - 1])
+    def bytes_of(kib):
+        return ig_ref.at[0, :, pl.ds(0, 2 * kib)]
+
+    def sent(sem, kib):
+        remote(bytes_of(kib), bytes_of(kib), sem, sem, pair).wait_send()
+
+    def arrived(sem, kib):
+        remote(bytes_of(kib), bytes_of(kib), sem, sem, pair).wait_recv()
+
+    def loaded(sem, kib):
+        pltpu.make_async_copy(bytes_of(kib), bytes_of(kib), sem).wait()
 
     half_of = {UP: (0, 1), DOWN: (1, 0)}
 
@@ -168,28 +181,36 @@
         part = rows(h * HALF, HALF)
         return remote(
             rs_out.at[d, k - 1, part], rs_in.at[d, k - 1, part],
-            rs_s.at[d, k - 1, h], rs_r.at[d, k - 1, h], ring[d],
+            rs_s, rs_r.at[d, k - 1, h], ring[d],
         )
 
     def target(d, k):
         return k if d == UP else Z - k
 
+    def by_rows(start, size, step, action):
+        @pl.loop(0, size // step)
+        def _(i):
+            action(pl.ds(pl.multiple_of(start + i * step, step), step))
+
     def send_sum(d, k, h, chained):
-        part = rows(h * HALF, HALF)
-        total = term[target(d, k), part, :]
         if chained:
             reduce_copy(d, k + 1, h).wait_recv()
-            total = total + rs_in[d, k, part, :].astype(F32)
-        rs_out[d, k - 1, part, :] = total.astype(BF16)
+
+        def add(part):
+            total = term[target(d, k), part, :]
+            if chained:
+                total = total + rs_in[d, k, part, :].astype(F32)
+            rs_out[d, k - 1, part, :] = total.astype(BF16)
+
+        by_rows(h * HALF, HALF, 32, add)
         reduce_copy(d, k, h).start()
 
     def make_term(s):
-        own_x[s].wait()
         y_x[s].wait_recv()
 
-        @pl.loop(0, ROWS // 256)
+        @pl.loop(0, ROWS // 128)
         def _(i):
-            part = pl.ds(pl.multiple_of(i * 256, 256), 256)
+            part = pl.ds(pl.multiple_of(i * 128, 128), 128)
             term[s, part, :] = lax.dot_general(
                 xin[s, :, part], cot[...], (((0,), (0,)), ((), ())), preferred_element_type=F32
             )
@@ -200,30 +221,30 @@
     def pair_columns(r, start, size):
         return pl.ds(pl.multiple_of(((1 - yl) * Z + lax.rem(z + Z - r, Z)) * ROWS + start, 128), size)
 
-    def far_part(r):
-        return (0, ROWS, ig_last) if r == 4 else (PURE, HYB, ig_far.at[r])
+    def far_start(r):
+        return 0 if r == 4 else PURE
 
     def ig_sent(r):
-        start, size, src = far_part(r)
+        start = far_start(r)
+        size = ROWS - start
         return remote(
-            src, ig_ref.at[0, :, own_columns(r, start, size)], yi_s.at[r], yi_r.at[r], pair
+            ig_far.at[r, :, pl.ds(start, size)], ig_ref.at[0, :, own_columns(r, start, size)],
+            y_s, yi_r, pair,
         )
-
-    def ig_arrival(r):
-        start, size, _ = far_part(r)
-        part = ig_ref.at[0, :, pair_columns(r, start, size)]
-        return remote(part, part, yi_s.at[r], yi_r.at[r], pair)
 
     def make_ig(r):
         transposed = (((1,), (1,)), ((), ()))
-        start, size, far_ref = far_part(r)
-        far_ref[...] = lax.dot_general(
-            cot[TOK:, :], wb[r, start:ROWS, :], transposed, preferred_element_type=F32
-        ).astype(BF16)
+
+        @pl.loop(0, ROWS // 128)
+        def _(i):
+            start = pl.multiple_of(i * 128, 128)
+            product = lax.dot_general(
+                cot[...], wb[r, pl.ds(start, 128), :], transposed, preferred_element_type=F32
+            ).astype(BF16)
+            ig_ref[0, :, own_columns(r, start, 128)] = product[:TOK]
+            ig_far[r, :, pl.ds(start, 128)] = product[TOK:]
+
         ig_sent(r).start()
-        ig_ref[0, :, own_columns(r, 0, ROWS)] = lax.dot_general(
-            cot[:TOK, :], wb[r, :ROWS, :], transposed, preferred_element_type=F32
-        ).astype(BF16)
         if r != 4:
             ig_ref[0, :, pair_columns(r, 0, PURE)] = lax.dot_general(
                 cot[:TOK, :], wb[r, ROWS:, :], transposed, preferred_element_type=F32
@@ -242,7 +263,7 @@
                 fourth_start(d, 2)
 
     pl.semaphore_wait(
-        barrier, 1 + count(z > 0) + count(z == Z - 1) + count(yl == 1) + count(isl != ROOT)
+        barrier, 1 + count(z > 0) + count(z == Z - 1) + count(yl == 1) + count(q != ROOT) + count(high_root)
     )
     pl.when(yl == 1)(lambda: greet(pair_in, pair))
     pl.when(z > 0)(lambda: greet(above, down))
@@ -260,7 +281,7 @@
         y_x[s].start()
     pl.when(z < Z - 1)(lambda: pl.semaphore_wait(above, 1))
     start_gather(UP)
-    pl.when(isl != ROOT)(lambda: greet(here, (ROOT, fs)))
+    pl.when(q != ROOT)(lambda: greet(here, root))
     for copy in local:
         copy.start()
     for s in (4, 3, 5, 2, 6, 1, 7, 0):
@@ -271,9 +292,14 @@
         pl.semaphore_wait(below, 1)
         start_gather(DOWN)
 
-    @pl.when(isl == ROOT)
+    @pl.when(high_root)
     def _():
-        pl.semaphore_wait(here, ISLANDS - 1)
+        pl.semaphore_wait(here, PLANE - 1)
+        greet(here, far)
+
+    @pl.when(low_root)
+    def _():
+        pl.semaphore_wait(here, PLANE)
         for j in range(1, ISLANDS):
             greet(all_in, (lax.rem(isl + j, ISLANDS), fs))
 
@@ -287,13 +313,17 @@
     for d in (UP, DOWN):
         gather(d, 0, 2).start()
     pass_on(0, 0)
-    for copy in local[:3]:
-        copy.wait()
-    total = pg_own[...].astype(F32)
-    for j in range(1, PLANE):
-        c_1[j - 1].wait_recv()
-        total = total + c_in[j - 1].astype(F32)
-    c_out[...] = total.astype(BF16)
+    loaded(lm, 256 + 512 + 64 + 1024 + 1024)
+    loaded(lx, 8 * 256)
+    arrived(c1_r, 7 * 64)
+
+    def plane_sum(part):
+        total = pg_own[part, :].astype(F32)
+        for j in range(1, PLANE):
+            total = total + c_in[j - 1, part, :].astype(F32)
+        c_out[part, :] = total.astype(BF16)
+
+    by_rows(0, PIECE, 16, plane_sum)
     c_2.start()
     for s in (6, 1, 7, 0):
         y_x[s].start()
@@ -339,62 +369,44 @@
         for d in (UP, DOWN):
             send_sum(d, 2, half_of[d][h], True)
 
-    for copy in local[3:]:
-        copy.wait()
-    for j in range(1, PLANE):
-        c_3_arrival(j).wait_recv()
-
-    @pl.loop(0, ROWS // 64)
-    def _(i):
-        part = pl.ds(pl.multiple_of(i * 64, 64), 64)
+    arrived(c3_r, 7 * 128)
+
+    def update(part):
         average = avg[part, :]
         momentum = outer_beta * omb[part, :] + average
         nm_ref[part, :] = momentum
         np_ref[part, :] = opb[part, :] - outer_rate * (average + outer_beta * momentum)
 
+    by_rows(0, ROWS, 16, update)
+
     for h in (1, 0):
         for d in (UP, DOWN):
             send_sum(d, 1, half_of[d][h], True)
 
-    y_w.wait_send()
-    y_c.wait_send()
-    c_2.wait_send()
-    for s in range(Z):
-        y_x[s].wait_send()
-    for j in range(1, PLANE):
-        c_1[j - 1].wait_send()
-        c_3[j - 1].wait_send()
-    for d in (UP, DOWN):
-        for r in range(3):
-            for c in range(3):
-                gather(d, r, c).wait_send()
+    sent(c1_s, 7 * 64)
+    sent(c3_s, 7 * 128)
+    sent(ag_s, 2 * 3 * (ROWS + PURE))
+    for d in (UP, DOWN):
         for c in range(3):
             only(last_hop[d][c][2], fourth(d, c).wait_send)
-        reduce_copy(d, 4, half_of[d][0]).wait_send()
-        for k in (3, 2):
-            for h in (0, 1):
-                reduce_copy(d, k, h).wait_send()
-    for r in (0, 1, 7, 2, 6):
-        ig_sent(r).wait_send()
-        ig_arrival(r).wait_recv()
 
     for last in (False, True):
         for d in (UP, DOWN):
             h = half_of[d][0 if last else 1]
             reduce_copy(d, 1, h).wait_recv()
-            part = rows(h * HALF, HALF)
-            arrived = rs_in[d, 0, part, :].astype(F32)
-            if last:
-                wg_ref[0, part, :] = (wg_ref[0, part, :] + arrived) * (1.0 / 4096)
-            else:
-                wg_ref[0, part, :] = term[0, part, :] + arrived
-
-    for d in (UP, DOWN):
-        for h in (0, 1):
-            reduce_copy(d, 1, h).wait_send()
-    for r in (3, 5, 4):
-        ig_sent(r).wait_send()
-        ig_arrival(r).wait_recv()
+
+            def add(part):
+                arrived = rs_in[d, 0, part, :].astype(F32)
+                if last:
+                    wg_ref[0, part, :] = (wg_ref[0, part, :] + arrived) * (1.0 / 4096)
+                else:
+                    wg_ref[0, part, :] = term[0, part, :] + arrived
+
+            by_rows(h * HALF, HALF, 32, add)
+
+    sent(rs_s, 2 * 7 * HALF)
+    sent(y_s, PURE + TOK + 8 * TOK + PIECE + 7 * (TOK * 3 // 4) + TOK)
+    arrived(yi_r, 7 * (TOK * 3 // 4) + TOK)
 
 
 def finish_kernel(a, b, c, d, a_out, b_out, c_out, d_out, sems):
@@ -440,8 +452,7 @@
             vmem((Z, ROWS, KW), F32),
             vmem((2, 4, ROWS, KW), BF16),
             vmem((2, 4, ROWS, KW), BF16),
-            vmem((Z, TOK, HYB), BF16),
-            vmem((TOK, ROWS), BF16),
+            vmem((Z, TOK, ROWS), BF16),
             vmem((PIECE, KW), BF16),
             vmem((PLANE - 1, PIECE, KW), BF16),
             vmem((PIECE, KW), BF16),
@@ -449,15 +460,9 @@
             vmem((ROWS, KW), F32),
             vmem((ROWS, KW), F32),
             vmem((ROWS, KW), F32),
-            dma((2, 4, 3)), dma((2, 4, 3)),
-            dma((2, 4, 2)), dma((2, 4, 2)),
-            dma((Z,)), dma((Z,)),
-            dma, dma, dma, dma,
-            dma((Z,)), dma((Z,)),
-            dma((PLANE - 1,)), dma((PLANE - 1,)),
-            dma, dma,
-            dma((PLANE - 1,)), dma((PLANE - 1,)),
-            dma((Z,)), dma((5,)),
+            dma, dma, dma((2, 3)), dma, dma, dma,
+            dma((2, 4, 3)), dma((2, 4, 2)), dma((Z,)), dma, dma,
+            dma, dma, dma, dma, dma, dma,
         ]
         + [pltpu.SemaphoreType.REGULAR] * 5,
         compiler_params=pltpu.CompilerParams(

time: 99.5 us -> 98.7 us (level)
  no operation moved by 1% of the time
where the time goes in v6:
time: 98.7 us; the launch traced here: 97.7 us
  Pallas kernels  97 us (98%)
    pallas_call x1, Pallas kernels, body(): pl.pallas_call(kernel, name='key_backward', out_shape=(vmem((1, TOK, 2 *...  94 us
    pallas_call x1, Pallas kernels, finish(): pl.pallas_call(finish_kernel, name='finish', out_shape=tuple((jax.ShapeDt...  3.02 us

profile of v6, /device:TPU:1, one launch (start us, length us, event | category | flops | bytes accessed | tf_op | source)
XLA Modules:
  0.0 97.7 jit_solution(13165205410861272348)
XLA Ops:
  0.6 94.0 %key_backward.1 = (bf16[1,256,8192]{2,1,0:T(8,128)(2,1)S(1)}, f32[1,512,512]{2,1,0:T(8,128)S(1)}, f32[512,512]{1,0:T(8,128)S(1)}, f32[512,512]{1,0:T(8,128)S(1)}) custom-call(bf16[1,256,8192]{2,1,0:T(8,128)(2,1)} %x_ref.1, bf16[1,256,512]{2,1,0:T(8,128)(2,1)} %c_ref.1, bf16[1,512,512]{2,1,0:T(8,128)(2,1)} %w_ref.1, bf16[1,512,512]{2,1,0:T(8,128)(2,1)} %pg_ref.1, ...), custom_call_target="tpu_custom_call" | custom-call | flops 4294967296 | bytes 25165824 | tf_op jit(solution)/shard_map/key_backward/pallas_call | solution.py:437
  94.7 3.0 %finish.1 = (bf16[1,256,8192]{2,1,0:T(8,128)(2,1)}, f32[1,512,512]{2,1,0:T(8,128)}, f32[512,512]{1,0:T(8,128)}, f32[512,512]{1,0:T(8,128)}) custom-call(bf16[1,256,8192]{2,1,0:T(8,128)(2,1)S(1)} %get-tuple-element.8.a, f32[1,512,512]{2,1,0:T(8,128)S(1)} %get-tuple-element.9.b, f32[512,512]{1,0:T(8,128)S(1)} %get-tuple-element.10.c, ...), custom_call_target="tpu_custom_call" | custom-call | tf_op jit(solution)/shard_map/finish/pallas_call | solution.py:422

commit v7 on v6

--- a/solution.py
+++ b/solution.py
@@ -39,8 +39,8 @@
     cot, xin, wb, term, rs_in, rs_out, ig_far,
     pg_own, c_in, c_out, c_far, avg, opb, omb,
     y_s, ag_s, ag4_s, rs_s, c1_s, c3_s,
-    ag_r, rs_r, yx_r, yc_r, yw_r, yi_r, c1_r, c2_r, c3_r,
-    lx, lm, above, below, pair_in, here, all_in,
+    ag_r, ag4_r, rs_r, yx_r, yc_r, yw_r, yi_r, c1_r, c2_r, c3_r,
+    lx, lm, above, below, here, all_in,
 ):
     isl = lax.axis_index("island")
     fs = lax.axis_index("fsdp")
@@ -57,7 +57,7 @@
     def greet(sem, peer):
         pl.semaphore_signal(sem, inc=1, device_id=peer, device_id_type=MESH)
 
-    pl.when(yl == 0)(lambda: greet(barrier, pair))
+    greet(barrier, pair)
     greet(barrier, (isl, fs))
     pl.when(z < Z - 1)(lambda: greet(barrier, up))
     pl.when(z == 0)(lambda: greet(barrier, down))
@@ -116,20 +116,20 @@
         start, size = cuts[c]
         src = w_ref.at[0, rows(start, size)] if r == 0 and c < 2 else wb.at[slot(d, r), rows(start, size)]
         dst = wb.at[slot(d, r + 1), rows(start, size)]
-        return remote(src, dst, ag_s, ag_r.at[d, r, c], ring[d])
+        return remote(src, dst, ag_s, ag_r.at[d, r, 0 if c == first[d] else 1], ring[d])
 
     first = {UP: 0, DOWN: 1}
 
     last_hop = {
         UP: (
-            (0, HALF - SIDE, None, None),
-            (HALF - SIDE, SIDE, z < Z - 1, z > 0),
-            (HALF, SIDE, z == Z - 2, z == Z - 1),
+            (0, HALF - SIDE, None),
+            (HALF - SIDE, SIDE, z < Z - 1),
+            (HALF, SIDE, z == Z - 2),
         ),
         DOWN: (
-            (HALF + SIDE, HALF - SIDE, None, None),
-            (HALF, SIDE, z > 0, z < Z - 1),
-            (HALF - SIDE, SIDE, z == 1, z == 0),
+            (HALF + SIDE, HALF - SIDE, None),
+            (HALF, SIDE, z > 0),
+            (HALF - SIDE, SIDE, z == 1),
         ),
     }
 
@@ -137,7 +137,7 @@
         start, size = last_hop[d][c][:2]
         return remote(
             wb.at[slot(d, 3), rows(start, size)], wb.at[4, rows(start, size)],
-            ag4_s.at[d, c], ag_r.at[d, 3, c], ring[d],
+            ag4_s, ag4_r, ring[d],
         )
 
     def only(condition, action):
@@ -181,7 +181,7 @@
         part = rows(h * HALF, HALF)
         return remote(
             rs_out.at[d, k - 1, part], rs_in.at[d, k - 1, part],
-            rs_s, rs_r.at[d, k - 1, h], ring[d],
+            rs_s, rs_r.at[d, 6 if k == 4 else 2 * (k - 1) + h], ring[d],
         )
 
     def target(d, k):
@@ -252,20 +252,20 @@
 
     def pass_on(r, i):
         for d in (UP, DOWN):
-            c = 2 if i == 2 else (first[d] if i == 0 else 1 - first[d])
-            gather(d, r, c).wait_recv()
+            if i == 0:
+                gather(d, r, first[d]).wait_recv()
+            else:
+                arrived(ag_r.at[d, r, 1], HALF + PURE)
             if r + 1 < 3:
-                gather(d, r + 1, c).start()
-            elif i == 0:
-                fourth_start(d, 0)
-                fourth_start(d, 1)
-            elif i == 1:
-                fourth_start(d, 2)
+                for c in (first[d],) if i == 0 else (1 - first[d], 2):
+                    gather(d, r + 1, c).start()
+            else:
+                for c in (0, 1) if i == 0 else (2,):
+                    fourth_start(d, c)
 
     pl.semaphore_wait(
-        barrier, 1 + count(z > 0) + count(z == Z - 1) + count(yl == 1) + count(q != ROOT) + count(high_root)
+        barrier, 2 + count(z > 0) + count(z == Z - 1) + count(q != ROOT) + count(high_root)
     )
-    pl.when(yl == 1)(lambda: greet(pair_in, pair))
     pl.when(z > 0)(lambda: greet(above, down))
     pl.when(z == Z - 1)(lambda: greet(below, up))
 
@@ -273,7 +273,6 @@
         gather(d, 0, first[d]).start()
         gather(d, 0, 1 - first[d]).start()
 
-    pl.when(yl == 0)(lambda: pl.semaphore_wait(pair_in, 1))
     y_w.start()
     y_c.start()
     pl.when(z > 0)(lambda: start_gather(DOWN))
@@ -330,15 +329,13 @@
     y_c.wait_recv()
     make_ig(0)
     pass_on(0, 1)
-    pass_on(0, 2)
     make_term(4)
     make_ig(1)
     make_ig(7)
     pass_on(1, 0)
     make_term(3)
+    make_term(5)
     pass_on(1, 1)
-    make_term(5)
-    pass_on(1, 2)
     make_ig(2)
     make_ig(6)
     make_term(2)
@@ -349,7 +346,6 @@
         copy.start()
     make_term(6)
     pass_on(2, 1)
-    pass_on(2, 2)
     for d in (UP, DOWN):
         send_sum(d, 4, half_of[d][0], False)
     for d in (UP, DOWN):
@@ -357,9 +353,7 @@
     make_ig(3)
     make_ig(5)
     make_term(1)
-    for d in (UP, DOWN):
-        for c in range(3):
-            only(last_hop[d][c][3], fourth(d, c).wait_recv)
+    arrived(ag4_r, ROWS)
     make_ig(4)
     make_term(7)
     for d in (UP, DOWN):
@@ -386,9 +380,15 @@
     sent(c1_s, 7 * 64)
     sent(c3_s, 7 * 128)
     sent(ag_s, 2 * 3 * (ROWS + PURE))
-    for d in (UP, DOWN):
-        for c in range(3):
-            only(last_hop[d][c][2], fourth(d, c).wait_send)
+    def fourth_sent(size):
+        part = wb.at[0, rows(0, size)]
+        remote(part, part, ag4_s, ag4_s, pair).wait_send()
+
+    less = (z == 0) | (z == Z - 1)
+    more = (z == 1) | (z == Z - 2)
+    pl.when(less)(lambda: fourth_sent(ROWS - SIDE))
+    pl.when(more)(lambda: fourth_sent(ROWS + SIDE))
+    pl.when(jnp.logical_not(less | more))(lambda: fourth_sent(ROWS))
 
     for last in (False, True):
         for d in (UP, DOWN):
@@ -460,11 +460,11 @@
             vmem((ROWS, KW), F32),
             vmem((ROWS, KW), F32),
             vmem((ROWS, KW), F32),
-            dma, dma, dma((2, 3)), dma, dma, dma,
-            dma((2, 4, 3)), dma((2, 4, 2)), dma((Z,)), dma, dma,
+            dma, dma, dma, dma, dma, dma,
+            dma((2, 3, 2)), dma, dma((2, 7)), dma((Z,)), dma, dma,
             dma, dma, dma, dma, dma, dma,
         ]
-        + [pltpu.SemaphoreType.REGULAR] * 5,
+        + [pltpu.SemaphoreType.REGULAR] * 4,
         compiler_params=pltpu.CompilerParams(
             collective_id=0, has_side_effects=True, vmem_limit_bytes=54 * 2**20
         ),

time: 98.7 us -> 98.5 us (level); the launches traced: 97.7 us -> 98.5 us
  no operation moved by 1% of the time
where the time goes in v7:
time: 98.5 us
  Pallas kernels  97.8 us (99%)
    pallas_call x1, Pallas kernels, body(): pl.pallas_call(kernel, name='key_backward', out_shape=(vmem((1, TOK, 2 *...  94.8 us
    pallas_call x1, Pallas kernels, finish(): pl.pallas_call(finish_kernel, name='finish', out_shape=tuple((jax.ShapeDt...  3.02 us

profile of v7, /device:TPU:1, one launch (start us, length us, event | category | flops | bytes accessed | tf_op | source)
XLA Modules:
  0.0 98.5 jit_solution(18234741607239254119)
XLA Ops:
  0.6 94.8 %key_backward.1 = (bf16[1,256,8192]{2,1,0:T(8,128)(2,1)S(1)}, f32[1,512,512]{2,1,0:T(8,128)S(1)}, f32[512,512]{1,0:T(8,128)S(1)}, f32[512,512]{1,0:T(8,128)S(1)}) custom-call(bf16[1,256,8192]{2,1,0:T(8,128)(2,1)} %x_ref.1, bf16[1,256,512]{2,1,0:T(8,128)(2,1)} %c_ref.1, bf16[1,512,512]{2,1,0:T(8,128)(2,1)} %w_ref.1, bf16[1,512,512]{2,1,0:T(8,128)(2,1)} %pg_ref.1, ...), custom_call_target="tpu_custom_call" | custom-call | flops 4294967296 | bytes 25165824 | tf_op jit(solution)/shard_map/key_backward/pallas_call | solution.py:437
  95.4 3.0 %finish.1 = (bf16[1,256,8192]{2,1,0:T(8,128)(2,1)}, f32[1,512,512]{2,1,0:T(8,128)}, f32[512,512]{1,0:T(8,128)}, f32[512,512]{1,0:T(8,128)}) custom-call(bf16[1,256,8192]{2,1,0:T(8,128)(2,1)S(1)} %get-tuple-element.8.a, f32[1,512,512]{2,1,0:T(8,128)S(1)} %get-tuple-element.9.b, f32[512,512]{1,0:T(8,128)S(1)} %get-tuple-element.10.c, ...), custom_call_target="tpu_custom_call" | custom-call | tf_op jit(solution)/shard_map/finish/pallas_call | solution.py:422

commit v8 on v7

--- a/solution.py
+++ b/solution.py
@@ -25,7 +25,7 @@
 
 UP, DOWN = 0, 1
 ISLANDS = 2 * PLANE
-SIDE = 96
+SIDE = 80
 ROOT = 1
 
 
@@ -266,6 +266,8 @@
     pl.semaphore_wait(
         barrier, 2 + count(z > 0) + count(z == Z - 1) + count(q != ROOT) + count(high_root)
     )
+    y_w.start()
+    y_c.start()
     pl.when(z > 0)(lambda: greet(above, down))
     pl.when(z == Z - 1)(lambda: greet(below, up))
 
@@ -273,8 +275,6 @@
         gather(d, 0, first[d]).start()
         gather(d, 0, 1 - first[d]).start()
 
-    y_w.start()
-    y_c.start()
     pl.when(z > 0)(lambda: start_gather(DOWN))
     for s in (4, 3, 5, 2):
         y_x[s].start()

time: 98.5 us -> 98.2 us (level)
  no operation moved by 1% of the time
where the time goes in v8:
time: 98.2 us; the launch traced here: 98.1 us
  Pallas kernels  97.5 us (99%)
    pallas_call x1, Pallas kernels, body(): pl.pallas_call(kernel, name='key_backward', out_shape=(vmem((1, TOK, 2 *...  94.4 us
    pallas_call x1, Pallas kernels, finish(): pl.pallas_call(finish_kernel, name='finish', out_shape=tuple((jax.ShapeDt...  3.02 us

profile of v8, /device:TPU:1, one launch (start us, length us, event | category | flops | bytes accessed | tf_op | source)
XLA Modules:
  0.0 98.1 jit_solution(9472804890863836155)
XLA Ops:
  0.6 94.4 %key_backward.1 = (bf16[1,256,8192]{2,1,0:T(8,128)(2,1)S(1)}, f32[1,512,512]{2,1,0:T(8,128)S(1)}, f32[512,512]{1,0:T(8,128)S(1)}, f32[512,512]{1,0:T(8,128)S(1)}) custom-call(bf16[1,256,8192]{2,1,0:T(8,128)(2,1)} %x_ref.1, bf16[1,256,512]{2,1,0:T(8,128)(2,1)} %c_ref.1, bf16[1,512,512]{2,1,0:T(8,128)(2,1)} %w_ref.1, bf16[1,512,512]{2,1,0:T(8,128)(2,1)} %pg_ref.1, ...), custom_call_target="tpu_custom_call" | custom-call | flops 4294967296 | bytes 25165824 | tf_op jit(solution)/shard_map/key_backward/pallas_call | solution.py:437
  95.1 3.0 %finish.1 = (bf16[1,256,8192]{2,1,0:T(8,128)(2,1)}, f32[1,512,512]{2,1,0:T(8,128)}, f32[512,512]{1,0:T(8,128)}, f32[512,512]{1,0:T(8,128)}) custom-call(bf16[1,256,8192]{2,1,0:T(8,128)(2,1)S(1)} %get-tuple-element.8.a, f32[1,512,512]{2,1,0:T(8,128)S(1)} %get-tuple-element.9.b, f32[512,512]{1,0:T(8,128)S(1)} %get-tuple-element.10.c, ...), custom_call_target="tpu_custom_call" | custom-call | tf_op jit(solution)/shard_map/finish/pallas_call | solution.py:422
